TPU v7x, 512 devices: a whole 4x4x16 slice. The times are simulated.
512 devices in a mesh: ctx: 16 (over z), chan: 32 (over y, x, core).
Axes of the slice: x: 4, y: 4, z: 16, core: 2. Of those that a mesh axis runs over, the one named last changes fastest.
Arguments:
- conv_input: bfloat16 [2048, 16384], P('ctx', 'chan'), may hold values from -6 to 6
- gate_input: bfloat16 [2048, 16384], P('ctx', 'chan'), may hold values from -6 to 6
- out_grad: bfloat16 [2048, 16384], P('ctx', 'chan'), may hold values from -6 to 6
- conv_weight: float32 [4, 16384], P(None, 'chan'), may hold values from -3 to 3
- conv_bias: float32 [16384], P('chan'), may hold values from -3 to 3
- proj_weight: bfloat16 [544, 16384], P(None, 'chan'), may hold values from -0.046875 to 0.046875
- step_weight: bfloat16 [512, 16384], P(None, 'chan'), may hold values from -0.25 to 0.25
- step_bias: float32 [16384], P('chan'), may hold values from -12 to -3
- decay_log: float32 [16, 16384], P(None, 'chan'), may hold values from -0.7 to 1.4
- skip_gain: float32 [16384], P('chan'), may hold values from 0.1 to 1.9
Outputs:
- grad_input: bfloat16 [2048, 16384], P('ctx', 'chan')
- grad_gate: bfloat16 [2048, 16384], P('ctx', 'chan')
- grad_proj: float32 [512, 16384], P('ctx', 'chan')
- grad_coef: float32 [32, 16384], P('ctx', 'chan')
- grad_step: float32 [512, 16384], P('ctx', 'chan')
- grad_conv_weight: float32 [4, 16384], P(None, 'chan')
- grad_conv_bias: float32 [16384], P('chan')
- grad_step_bias: float32 [16384], P('chan')
- grad_decay_log: float32 [16, 16384], P(None, 'chan')
- grad_skip: float32 [16384], P('chan')
All inputs are finite; a program needn't handle non-finite values.
Results may differ from a plain program's by a relative error of at most 0.023.
Values may be sent and summed in bfloat16 or wider, within the bound.
A program may use at most 64 MiB of HBM per device.

v0:
```python
import functools

import jax
import jax.numpy as jnp
from jax import lax
from jax.experimental import pallas as pl
from jax.experimental.pallas import tpu as pltpu
from jax.sharding import PartitionSpec as P

LANE = 128
ROWS = 16
LOG2E = 1.4426950408889634
F32 = jnp.float32
BF16 = jnp.bfloat16
MESH = pl.DeviceIdType.MESH


def silu_slope(values):
    sigma = jax.nn.sigmoid(values)
    return sigma * (1.0 + values * (1.0 - sigma))


def dot(a, b, over_a, over_b):
    return lax.dot_general(
        a, b, (((over_a,), (over_b,)), ((), ())), preferred_element_type=F32
    )


def kernel(sizes, *refs):
    Z, Y, T, C, R, N, K = sizes
    CB = C // LANE
    nz = N // Z
    cr = 2 * N // Y
    rz = R // Z
    L = Z // 2
    M = Z - 1 - L
    nb = T // ROWS
    (
        x_h, gate_h, og_h, cw_h, cb_h, pw_h, sw_h, sb_h, dl_h, sk_h,
        gin_o, ggate_o, gproj_o, gcoef_o, gstep_o, gcw_o, gcb_o, gsb_o, gdl_o, gsk_o,
        x_v, gate_v, og_v, cw_v, cb_v, pw_v, sw_v, sb_v, dl_v, sk_v,
        halo_v, xe_v, slope_v, co_v, cv_v, sbuf, rbuf, gbuf, ct_v, bc_v,
        st_v, sig_v, dr_v, g_v, gg_v, sp_v, stot_v, a2_v, a3_v, f_v, hist_v,
        ebuf, erecv, obuf, pbuf, sin_v, cin_v, so_v, dd_v, ab_v, pre_v, cg_v, dg_v,
        gs_v, gp_v, gc_v, bct_v, dc_v, halo2_v, oth_v, mbuf, mrecv, ag_v,
        lsend, lrecv, msend, mrcv2,
        lsem, hs, hr, h2s, h2r, s1, r1, s2, r2, s3, r3, s4, r4,
        ss_s, ss_r, se_s, se_r, sp_s, sp_r, sm_s, sm_r, sg_s, sg_r,
        ls_s, ls_r, ms_s, ms_r,
    ) = refs
    z = lax.axis_index("ctx")
    c = lax.axis_index("chan")
    nxt = lax.rem(z + 1, Z)
    prv = lax.rem(z + Z - 1, Z)

    def remote(src, dst, send, recv, device):
        return pltpu.make_async_remote_copy(
            src_ref=src, dst_ref=dst, send_sem=send, recv_sem=recv,
            device_id=device, device_id_type=MESH,
        )

    def settle(ref, sem):
        pltpu.make_async_copy(ref, ref, sem).wait()

    def to_peers(axis, count, me, src_of, dst, send, recv):
        @pl.loop(1, count)
        def _(k):
            peer = lax.rem(me + k, count)
            remote(src_of(peer), dst, send, recv, {axis: peer}).start()

    pairs = (
        (x_h, x_v), (cw_h, cw_v), (cb_h, cb_v), (pw_h, pw_v), (gate_h, gate_v),
        (og_h, og_v), (sw_h, sw_v), (sb_h, sb_v), (dl_h, dl_v), (sk_h, sk_v),
    )
    loads = [pltpu.make_async_copy(a, b, lsem.at[i]) for i, (a, b) in enumerate(pairs)]
    for load in loads:
        load.start()
    barrier = pltpu.get_barrier_semaphore()

    @pl.loop(1, Z)
    def _(k):
        pl.semaphore_signal(
            barrier, inc=1, device_id={"ctx": lax.rem(z + k, Z)}, device_id_type=MESH
        )

    @pl.loop(1, Y)
    def _(k):
        pl.semaphore_signal(
            barrier, inc=1, device_id={"chan": lax.rem(c + k, Y)}, device_id_type=MESH
        )

    for load in loads[:4]:
        load.wait()
    pl.semaphore_wait(barrier, Z - 1 + Y - 1)

    halo = remote(x_v.at[pl.ds(T - ROWS, ROWS)], halo_v, hs, hr, {"ctx": nxt})
    halo.start()
    xe_v[ROWS:, :] = x_v[...].astype(F32)
    halo.wait_recv()
    xe_v[0:ROWS, :] = jnp.where(z == 0, 0.0, halo_v[...].astype(F32))

    @pl.loop(0, nb)
    def _(b):
        base = pl.multiple_of(b * ROWS, ROWS)
        window = xe_v[pl.ds(base, 2 * ROWS), :]
        pre = jnp.broadcast_to(cb_v[...], (ROWS, C))
        for k in range(K):
            first = ROWS - (K - 1) + k
            pre = pre + cw_v[k : k + 1, :] * window[first : first + ROWS]
        sigma = jax.nn.sigmoid(pre)
        out = (pre * sigma).astype(BF16)
        co_v[pl.ds(base, ROWS), :] = out
        cv_v[pl.ds(base, ROWS), :] = out.astype(F32)
        slope_v[pl.ds(base, ROWS), :] = sigma * (1.0 + pre * (1.0 - sigma))

    def pack(product, coefs):
        for d in range(Y):
            sbuf[d, 0:ROWS, :] = product[ROWS * d : ROWS * (d + 1)].astype(BF16)
            row = coefs[cr * d : cr * (d + 1)]
            if cr == 1:
                row = jnp.broadcast_to(row, (ROWS, LANE))
            else:
                row = jnp.concatenate([row] * (ROWS // cr), axis=0)
            sbuf[d, ROWS : 2 * ROWS, :] = row.astype(BF16)
        rbuf[c] = sbuf[c]

    def scatter_start(send, recv):
        to_peers("chan", Y, c, lambda d: sbuf.at[d], rbuf.at[c], send, recv)

    def reduce_and_spread(send, recv, gsend, grecv):
        settle(rbuf.at[pl.ds(0, Y - 1)], recv)
        total = lax.fori_loop(
            0, Y, lambda s, a: a + rbuf[s].astype(F32), jnp.zeros((2 * ROWS, LANE), F32),
            unroll=4,
        )
        gbuf[c] = total.astype(BF16)
        to_peers("chan", Y, c, lambda d: gbuf.at[c], gbuf.at[c], gsend, grecv)
        settle(sbuf.at[pl.ds(0, Y - 1)], send)

    def spread_finish(gsend, grecv):
        settle(gbuf.at[pl.ds(0, Y - 1)], grecv)
        for d in range(Y):
            rows = gbuf[d, ROWS : 2 * ROWS, :].astype(F32)
            ct_v[cr * d : cr * (d + 1), :] = rows[0:cr]
        settle(gbuf.at[pl.ds(0, Y - 1)], gsend)

    pack(
        dot(pw_v[0:R, :], co_v[...], 1, 1),
        dot(pw_v[R : R + 2 * N, :], co_v[...], 1, 1),
    )
    scatter_start(s1, r1)

    for load in loads[4:]:
        load.wait()

    @pl.loop(0, nb)
    def _(b):
        rows = pl.ds(pl.multiple_of(b * ROWS, ROWS), ROWS)
        gate = gate_v[rows, :].astype(F32)
        grad = og_v[rows, :].astype(F32)
        sigma = jax.nn.sigmoid(gate)
        g_v[rows, :] = grad * (gate * sigma)
        gg_v[rows, :] = grad * (sigma * (1.0 + gate * (1.0 - sigma)))

    a2 = -jnp.exp(dl_v[...])
    a2_v[...] = a2
    for n in range(N):
        for l in range(CB):
            a3_v[n, l : l + 1, :] = a2[n : n + 1, LANE * l : LANE * (l + 1)] * LOG2E

    reduce_and_spread(s1, r1, s2, r2)
    spread_finish(s2, r2)

    slt = gbuf[:, 0:ROWS, :].reshape(R, T)
    sp_v[...] = dot(slt, sw_v[...], 0, 0)

    def sizes_block(b, carry):
        size_sum, skip_sum = carry
        rows = pl.ds(pl.multiple_of(b * ROWS, ROWS), ROWS)
        pre = sp_v[rows, :] + sb_v[...]
        size = jnp.maximum(pre, 0.0) + jnp.log1p(jnp.exp(-jnp.abs(pre)))
        st_v[rows, :] = size
        sig_v[rows, :] = jax.nn.sigmoid(pre)
        conv = cv_v[rows, :]
        dr_v[rows, :] = size * conv
        size_sum = size_sum + jnp.sum(size, axis=0, keepdims=True)
        skip_sum = skip_sum + jnp.sum(g_v[rows, :] * conv, axis=0, keepdims=True)
        return size_sum, skip_sum

    size_sum, skip_sum = lax.fori_loop(
        0, nb, sizes_block, (jnp.zeros((1, C), F32), jnp.zeros((1, C), F32))
    )
    oth_v[...] = jnp.zeros_like(oth_v)
    oth_v[K + 2 : K + 3, :] = skip_sum
    for l in range(CB):
        stot_v[z, l : l + 1, :] = size_sum[:, LANE * l : LANE * (l + 1)]
    to_peers("ctx", Z, z, lambda p: stot_v.at[z], stot_v.at[z], ss_s, ss_r)

    U = 8

    def forward_local(b, h):
        shift = lax.rem(T - b * U, T)
        turned = pltpu.roll(ct_v[...], shift, 1)
        a2s = a2_v[...] * LOG2E
        for i in range(U):
            t = b * U + i
            cols = jnp.broadcast_to(turned[:, i : i + 1], (2 * N, LANE))
            bc_v[t] = cols
            size = st_v[pl.ds(t, 1), :]
            drive = dr_v[pl.ds(t, 1), :]
            f = jnp.exp2(size * a2s)
            f_v[t] = f
            h = f * h + drive * jnp.concatenate([cols[0:N]] * CB, axis=1)
        return h

    end = lax.fori_loop(0, T // U, forward_local, jnp.zeros((N, C), F32))

    def backward_local(b, q):
        for i in range(U):
            t = T - 1 - (b * U + i)
            coef = bc_v[t, N : 2 * N, :]
            q = f_v[t] * (jnp.concatenate([coef] * CB, axis=1) * g_v[pl.ds(t, 1), :] + q)
        return q

    head = lax.fori_loop(0, T // U, backward_local, jnp.zeros((N, C), F32))

    for n in range(N):
        p, i = divmod(n, nz)
        for l in range(CB):
            lanes = slice(LANE * l, LANE * (l + 1))
            ebuf[p, (2 * i) * CB + l : (2 * i) * CB + l + 1, :] = end[n : n + 1, lanes]
            ebuf[p, (2 * i + 1) * CB + l : (2 * i + 1) * CB + l + 1, :] = head[n : n + 1, lanes]
    erecv[z] = ebuf[z]
    to_peers("ctx", Z, z, lambda p: ebuf.at[p], erecv.at[z], se_s, se_r)
    settle(stot_v.at[pl.ds(0, Z - 1)], ss_r)
    settle(stot_v.at[pl.ds(0, Z - 1)], ss_s)
    decays = []
    for i in range(nz):
        rate = a3_v[z * nz + i][0:CB]
        decays.append([jnp.exp2(rate * stot_v[d][0:CB]) for d in range(Z)])
    settle(erecv.at[pl.ds(0, Z - 1)], se_r)
    for i in range(nz):
        top = slice(2 * i * CB, (2 * i + 1) * CB)
        low = slice((2 * i + 1) * CB, (2 * i + 2) * CB)
        state = jnp.zeros((CB, LANE), F32)
        for d in range(Z):
            obuf[d, top, :] = state
            state = erecv[d, top, :] + decays[i][d] * state
        state = jnp.zeros((CB, LANE), F32)
        for d in reversed(range(Z)):
            obuf[d, low, :] = state
            state = erecv[d, low, :] + decays[i][d] * state
    pbuf[z] = obuf[z]
    to_peers("ctx", Z, z, lambda p: obuf.at[p], pbuf.at[z], sp_s, sp_r)
    settle(ebuf.at[pl.ds(0, Z - 1)], se_s)
    settle(pbuf.at[pl.ds(0, Z - 1)], sp_r)
    for n in range(N):
        p, i = divmod(n, nz)
        for l in range(CB):
            lanes = slice(LANE * l, LANE * (l + 1))
            sin_v[n : n + 1, lanes] = pbuf[p, (2 * i) * CB + l : (2 * i) * CB + l + 1, :]
            cin_v[n : n + 1, lanes] = pbuf[p, (2 * i + 1) * CB + l : (2 * i + 1) * CB + l + 1, :]
    settle(obuf.at[pl.ds(0, Z - 1)], sp_s)

    lane = lax.broadcasted_iota(jnp.int32, (N, LANE), 1)

    def fold(wide):
        total = wide[:, 0:LANE]
        for l in range(1, CB):
            total = total + wide[:, LANE * l : LANE * (l + 1)]
        return jnp.sum(total, axis=1, keepdims=True)

    def forward_pass(b, carry):
        h, acc = carry
        for i in range(U):
            t = b * U + i
            cols = bc_v[t]
            drive = dr_v[pl.ds(t, 1), :]
            hist_v[t] = h
            h = f_v[t] * h + drive * jnp.concatenate([cols[0:N]] * CB, axis=1)
            out = jnp.concatenate([cols[N : 2 * N]] * CB, axis=1) * h
            so_v[pl.ds(t, 1), :] = jnp.sum(out, axis=0, keepdims=True)
            acc = jnp.where(lane == t, fold(h * g_v[pl.ds(t, 1), :]), acc)
        return h, acc

    _, coef_out = lax.fori_loop(
        0, T // U, forward_pass, (sin_v[...], jnp.zeros((N, LANE), F32))
    )

    def backward_pass(b, carry):
        q, acc, decay = carry
        a2w = a2_v[...]
        for i in range(U):
            t = T - 1 - (b * U + i)
            cols = bc_v[t]
            g = g_v[pl.ds(t, 1), :]
            adj = jnp.concatenate([cols[N : 2 * N]] * CB, axis=1) * g + q
            q = f_v[t] * adj
            w = q * hist_v[t]
            dd_v[pl.ds(t, 1), :] = jnp.sum(a2w * w, axis=0, keepdims=True)
            ab = jnp.concatenate([cols[0:N]] * CB, axis=1) * adj
            ab_v[pl.ds(t, 1), :] = jnp.sum(ab, axis=0, keepdims=True)
            decay = decay + w * st_v[pl.ds(t, 1), :]
            acc = jnp.where(lane == t, fold(adj * dr_v[pl.ds(t, 1), :]), acc)
        return q, acc, decay

    _, coef_in, decay = lax.fori_loop(
        0, T // U, backward_pass,
        (cin_v[...], jnp.zeros((N, LANE), F32), jnp.zeros((N, C), F32)),
    )
    dg_v[...] = decay * a2_v[...]

    def gate_block(b, bias_sum):
        rows = pl.ds(pl.multiple_of(b * ROWS, ROWS), ROWS)
        conv = cv_v[rows, :]
        g = g_v[rows, :]
        ab = ab_v[rows, :]
        skip = sk_v[...]
        pre = (dd_v[rows, :] + ab * conv) * sig_v[rows, :]
        pre_v[rows, :] = pre.astype(BF16)
        ggate_o[rows, :] = (gg_v[rows, :] * (so_v[rows, :] + skip * conv)).astype(BF16)
        cg_v[rows, :] = ab * st_v[rows, :] + skip * g
        return bias_sum + jnp.sum(pre, axis=0, keepdims=True)

    oth_v[K + 1 : K + 2, :] = lax.fori_loop(0, nb, gate_block, jnp.zeros((1, C), F32))

    pack(
        dot(sw_v[...], pre_v[...], 1, 1),
        jnp.concatenate([coef_in, coef_out], axis=0),
    )
    slt2 = gbuf[:, 0:ROWS, :].reshape(R, T)
    gs_v[...] = dot(slt2, pre_v[...], 1, 0).reshape(Z, rz, C)
    scatter_start(s3, r3)

    def ring(which, part, s):
        left, right = {"ctx": prv}, {"ctx": nxt}
        if s < L:
            value = part[lax.rem(z + Z - L + s, Z)]
            if s:
                settle(lrecv.at[which, s - 1], ls_r.at[which, s - 1])
                value = value + lrecv[which, s - 1].astype(F32)
            lsend[which, s] = value.astype(BF16)
            remote(
                lsend.at[which, s], lrecv.at[which, s],
                ls_s.at[which, s], ls_r.at[which, s], left,
            ).start()
        if s < M:
            value = part[lax.rem(z + M - s, Z)]
            if s:
                settle(mrcv2.at[which, s - 1], ms_r.at[which, s - 1])
                value = value + mrcv2[which, s - 1].astype(F32)
            msend[which, s] = value.astype(BF16)
            remote(
                msend.at[which, s], mrcv2.at[which, s],
                ms_s.at[which, s], ms_r.at[which, s], right,
            ).start()

    def ring_end(which, part):
        value = part[z]
        settle(lrecv.at[which, L - 1], ls_r.at[which, L - 1])
        value = value + lrecv[which, L - 1].astype(F32)
        if M:
            settle(mrcv2.at[which, M - 1], ms_r.at[which, M - 1])
            value = value + mrcv2[which, M - 1].astype(F32)
        for s in range(L):
            settle(lsend.at[which, s], ls_s.at[which, s])
        for s in range(M):
            settle(msend.at[which, s], ms_s.at[which, s])
        return value

    ring(0, gs_v, 0)
    ring(0, gs_v, 1)
    reduce_and_spread(s3, r3, s4, r4)
    ring(0, gs_v, 2)
    ring(0, gs_v, 3)
    spread_finish(s4, r4)

    bpt = gbuf[:, 0:ROWS, :].reshape(R, T)
    bct_v[...] = ct_v[...].astype(BF16)
    gp_v[...] = dot(bpt, co_v[...], 1, 0).reshape(Z, rz, C)
    ring(1, gp_v, 0)
    sp_v[...] = dot(bpt, pw_v[0:R, :], 0, 0) + dot(bct_v[...], pw_v[R : R + 2 * N, :], 0, 0)

    def conv_block(b, carry):
        base = pl.multiple_of(b * ROWS, ROWS)
        rows = pl.ds(base, ROWS)
        grad = (cg_v[rows, :] + sp_v[rows, :]) * slope_v[rows, :]
        dc_v[rows, :] = grad
        window = xe_v[pl.ds(base, 2 * ROWS), :]
        new = []
        for k in range(K):
            first = ROWS - (K - 1) + k
            taps = grad * window[first : first + ROWS]
            new.append(carry[k] + jnp.sum(taps, axis=0, keepdims=True))
        new.append(carry[K] + jnp.sum(grad, axis=0, keepdims=True))
        return tuple(new)

    sums = lax.fori_loop(0, nb, conv_block, (jnp.zeros((1, C), F32),) * (K + 1))
    halo2 = remote(dc_v.at[pl.ds(0, 8)], halo2_v, h2s, h2r, {"ctx": prv})
    halo2.start()
    for k in range(K + 1):
        oth_v[k : k + 1, :] = sums[k]
    gc_v[...] = dot(bct_v[...], co_v[...], 1, 0)
    ring(0, gs_v, 4)
    ring(1, gp_v, 1)

    other = 8 * CB // Z
    coef = 2 * N // Z
    for p in range(Z):
        at = 0
        for i in range(nz):
            for l in range(CB):
                n = p * nz + i
                mbuf[p, at : at + 1, :] = dg_v[n : n + 1, LANE * l : LANE * (l + 1)]
                at += 1
        for i in range(other):
            j, l = divmod(p * other + i, CB)
            mbuf[p, at : at + 1, :] = oth_v[j : j + 1, LANE * l : LANE * (l + 1)]
            at += 1
        for i in range(coef):
            for l in range(CB):
                n = p * coef + i
                mbuf[p, at : at + 1, :] = gc_v[n : n + 1, LANE * l : LANE * (l + 1)]
                at += 1
    mrecv[z] = mbuf[z]
    to_peers("ctx", Z, z, lambda p: mbuf.at[p], mrecv.at[z], sm_s, sm_r)

    halo2.wait_recv()
    dc_v[pl.ds(T, 8), :] = jnp.where(z == Z - 1, 0.0, halo2_v[...])

    @pl.loop(0, nb)
    def _(b):
        base = pl.multiple_of(b * ROWS, ROWS)
        window = dc_v[pl.ds(base, ROWS + 8), :]
        total = jnp.zeros((ROWS, C), F32)
        for k in range(K):
            lead = K - 1 - k
            total = total + cw_v[k : k + 1, :] * window[lead : lead + ROWS]
        gin_o[pl.ds(base, ROWS), :] = total.astype(BF16)

    ring(0, gs_v, 5)
    ring(1, gp_v, 2)
    settle(mrecv.at[pl.ds(0, Z - 1)], sm_r)
    total = mrecv[0]
    for d in range(1, Z):
        total = total + mrecv[d]
    shared = nz * CB + other
    ag_v[z] = total[0 : ag_v.shape[1]]
    to_peers("ctx", Z, z, lambda p: ag_v.at[z], ag_v.at[z], sg_s, sg_r)
    for i in range(coef):
        for l in range(CB):
            row = shared + i * CB + l
            gcoef_o[i : i + 1, LANE * l : LANE * (l + 1)] = total[row : row + 1]
    ring(0, gs_v, 6)
    ring(1, gp_v, 3)
    ring(0, gs_v, 7)
    ring(1, gp_v, 4)
    gstep_o[...] = ring_end(0, gs_v)
    ring(1, gp_v, 5)
    settle(ag_v.at[pl.ds(0, Z - 1)], sg_r)
    outs = [gcw_o.at[k : k + 1] for k in range(K)] + [gcb_o, gsb_o, gsk_o]
    for p in range(Z):
        at = 0
        for i in range(nz):
            for l in range(CB):
                n = p * nz + i
                gdl_o[n : n + 1, LANE * l : LANE * (l + 1)] = ag_v[p, at : at + 1, :]
                at += 1
        for i in range(other):
            j, l = divmod(p * other + i, CB)
            if j < len(outs):
                outs[j][:, LANE * l : LANE * (l + 1)] = ag_v[p, at : at + 1, :]
            at += 1
    ring(1, gp_v, 6)
    ring(1, gp_v, 7)
    gproj_o[...] = ring_end(1, gp_v)
    halo.wait_send()
    halo2.wait_send()
    settle(mbuf.at[pl.ds(0, Z - 1)], sm_s)
    settle(ag_v.at[pl.ds(0, Z - 1)], sg_s)


def body(sizes, *args):
    Z, Y, T, C, R, N, K = sizes
    conv_input, gate, og, cw, cb, pw, sw, sb, dl, sk = args
    CB = C // LANE
    nz = N // Z
    rz = R // Z
    L = Z // 2
    M = max(Z - 1 - L, 1)
    coef = 2 * N // Z
    other = 8 * CB // Z
    er = 2 * nz * CB
    small = -(-(nz * CB + other + coef * CB) // 8) * 8
    back = -(-(nz * CB + other) // 8) * 8
    vm = pltpu.VMEM
    dma = pltpu.SemaphoreType.DMA
    scratch = [
        vm((T, C), BF16), vm((T, C), BF16), vm((T, C), BF16), vm((K, C), F32), vm((1, C), F32),
        vm((R + 2 * N, C), BF16), vm((R, C), BF16), vm((1, C), F32), vm((N, C), F32), vm((1, C), F32),
        vm((ROWS, C), BF16), vm((T + ROWS, C), F32), vm((T, C), F32), vm((T, C), BF16), vm((T, C), F32),
        vm((Y, 2 * ROWS, LANE), BF16), vm((Y, 2 * ROWS, LANE), BF16), vm((Y, 2 * ROWS, LANE), BF16),
        vm((2 * N, T), F32), vm((T, 2 * N, LANE), F32),
        *[vm((T, C), F32) for _ in range(6)],
        vm((Z, 8, LANE), F32), vm((N, C), F32), vm((N, 8, LANE), F32), vm((T, N, C), F32), vm((T, N, C), F32),
        *[vm((Z, er, LANE), F32) for _ in range(4)], vm((N, C), F32), vm((N, C), F32),
        vm((T, C), F32), vm((T, C), F32), vm((T, C), F32), vm((T, C), BF16), vm((T, C), F32), vm((N, C), F32),
        vm((Z, rz, C), F32), vm((Z, rz, C), F32), vm((2 * N, C), F32), vm((2 * N, T), BF16),
        vm((T + 8, C), F32), vm((8, C), F32), vm((8, C), F32),
        vm((Z, small, LANE), F32), vm((Z, small, LANE), F32), vm((Z, back, LANE), F32),
        vm((2, L, rz, C), BF16), vm((2, L, rz, C), BF16), vm((2, M, rz, C), BF16), vm((2, M, rz, C), BF16),
        dma((10,)), *[dma(()) for _ in range(22)],
        dma((2, L)), dma((2, L)), dma((2, M)), dma((2, M)),
    ]
    shape = jax.ShapeDtypeStruct
    outs = pl.pallas_call(
        functools.partial(kernel, sizes),
        out_shape=[
            shape((T, C), BF16), shape((T, C), BF16), shape((rz, C), F32), shape((coef, C), F32),
            shape((rz, C), F32), shape((K, C), F32), shape((1, C), F32), shape((1, C), F32),
            shape((N, C), F32), shape((1, C), F32),
        ],
        in_specs=[pl.BlockSpec(memory_space=pl.ANY)] * 10,
        out_specs=[pl.BlockSpec(memory_space=pltpu.VMEM)] * 10,
        scratch_shapes=scratch,
        compiler_params=pltpu.CompilerParams(
            collective_id=0, has_side_effects=True, vmem_limit_bytes=48 * 2**20
        ),
    )(conv_input, gate, og, cw, cb[None], pw, sw, sb[None], dl, sk[None])
    flat = lambda a: a.reshape(-1)
    return (*outs[:6], flat(outs[6]), flat(outs[7]), outs[8], flat(outs[9]))


def solution(mesh):
    Z, Y = mesh.shape["ctx"], mesh.shape["chan"]

    def run(conv_input, *rest):
        cw, pw, sw, dl = rest[2], rest[4], rest[5], rest[7]
        sizes = (
            Z, Y, conv_input.shape[0] // Z, conv_input.shape[1] // Y,
            sw.shape[0], dl.shape[0], cw.shape[0],
        )
        return jax.shard_map(
            functools.partial(body, sizes), mesh=mesh, in_specs=in_specs, out_specs=out_specs,
            check_vma=False,
        )(conv_input, *rest)

    both, wide, flat = P("ctx", "chan"), P(None, "chan"), P("chan")
    in_specs = (both, both, both, wide, flat, wide, wide, flat, wide, flat)
    out_specs = (both, both, both, both, both, wide, flat, flat, wide, flat)
    return run
```

profile of v0, /device:TPU:2, one launch (start us, length us, event | category | flops | bytes accessed | tf_op | source)
XLA Modules:
  0.0 118.8 jit_solution(5146082183190340378)
XLA Ops:
  0.6 0.0 copy-start.8
  0.7 0.0 copy-start.7
  0.7 0.7 copy-done.8
  1.3 0.0 copy-done.7
  1.3 0.0 copy-start
  1.3 1.1 copy-done
  2.4 0.0 copy-start.1
  2.4 1.0 copy-done.1
  3.4 0.0 copy-start.2
  3.4 0.9 copy-done.2
  4.3 0.0 copy-start.3
  4.3 0.9 copy-done.3
  5.2 0.0 copy-start.4
  5.3 0.9 copy-done.4
  6.2 0.0 copy-start.5
  6.2 0.8 copy-done.5
  6.9 0.0 copy-start.6
  6.9 0.7 copy-done.6
  7.6 0.0 copy-start.9
  7.6 0.7 copy-done.9
  8.3 104.4 %shard_map.177 = (bf16[128,512]{1,0:T(8,128)(2,1)S(1)}, bf16[128,512]{1,0:T(8,128)(2,1)S(1)}, f32[32,512]{1,0:T(8,128)S(1)}, f32[2,512]{1,0:T(2,128)S(1)}, f32[3...) custom-call(bf16[128,512]{1,0:T(8,128)(2,1)S(1)} %copy-done.2, ...), custom_call_target="tpu_custom_call" | custom-call | tf_op jit(solution)/shard_map/pallas_call | solution.py:516
  112.7 0.7 copy.30
  113.4 0.7 copy.31
  114.0 0.6 copy.32
  114.7 0.6 copy.33
  115.3 0.6 copy.34
  115.9 0.6 copy.35
  116.5 0.6 copy.36
  117.1 0.6 copy.37
  117.7 0.6 copy.38
  118.3 0.6 copy.39
Async XLA Ops:
  0.6 0.7 copy-start.8
  0.7 0.7 copy-start.7
  1.3 1.1 copy-start
  2.4 1.0 copy-start.1
  3.4 0.9 copy-start.2
  4.3 0.9 copy-start.3
  5.2 0.9 copy-start.4
  6.2 0.8 copy-start.5
  6.9 0.7 copy-start.6
  7.6 0.7 copy-start.9
where the time goes:
time: 119 us
  Pallas kernels  104 us (87%)
  local copies, waits for them, and re-layouts  13.7 us (12%)
    pallas_call x1, Pallas kernels, body(): pl.pallas_call(functools.partial(kernel, sizes), out_shape=[shape((T, C),...  104 us
    unnamed x30, local copies, waits for them, and re-layouts  13.7 us

commit v1 on v0

v1 whole, which is shorter than its diff:
```python
import functools

import jax
import jax.numpy as jnp
from jax import lax
from jax.experimental import pallas as pl
from jax.experimental.pallas import tpu as pltpu
from jax.sharding import PartitionSpec as P

LANE = 128
ROWS = 16
LOG2E = 1.4426950408889634
VMEM_BYTES = 60 * 2**20
F32 = jnp.float32
BF16 = jnp.bfloat16
MESH = pl.DeviceIdType.MESH


def silu_slope(values):
    sigma = jax.nn.sigmoid(values)
    return sigma * (1.0 + values * (1.0 - sigma))


def dot(a, b, over_a, over_b):
    return lax.dot_general(
        a, b, (((over_a,), (over_b,)), ((), ())), preferred_element_type=F32
    )


def kernel(sizes, *refs):
    Z, Y, T, C, R, N, K = sizes
    CB = C // LANE
    nz = N // Z
    Q = Y // 2
    coef = 2 * N // Z
    rz = R // Z
    L = Z // 2
    M = Z - 1 - L
    nb = T // ROWS
    (
        x_h, gate_h, og_h, cw_h, cb_h, pw_h, sw_h, sb_h, dl_h, sk_h,
        gin_h, ggate_h, gproj_h, gcoef_h, gstep_h, gcw_h, gcb_h, gsb_h, gdl_h, gsk_h,
        gin_o, ggate_o, gproj_o, gcoef_o, gstep_o, gcw_o, gcb_o, gsb_o, gdl_o, gsk_o,
        x_v, gate_v, og_v, cw_v, cb_v, pw_v, sw_v, sb_v, dl_v, sk_v,
        halo_v, xe_v, slope_v, co_v, cv_v, sbuf, hbuf, tbuf, rbuf, gbuf, slt_v, ct_v, bc_v,
        st_v, sig_v, dr_v, g_v, gg_v, sp_v, stot_v, dec_v, a2_v, a3_v, f_v, hist_v,
        es_v, er_v, eo_v, ep_v, hs_v, hr_v, ho_v, hp_v, sin_v, cin_v,
        so_v, dd_v, ab_v, pre_v, cg_v, dg_v,
        gs_v, gp_v, gc_v, dc_v, halo2_v, oth_v, mf_v, mbuf, mrecv, ag_v, lsend, lrecv, msend, mrcv2,
        lsem, osem, hs, hr, h2s, h2r, ss_s, ss_r, es_s, es_r, ep_s, ep_r, hs_s, hs_r, hp_s, hp_r,
        sm_s, sm_r, sg_s, sg_r, send_sums, recv_sums, ls_s, ls_r, ms_s, ms_r,
    ) = refs
    outs_v = (gin_o, ggate_o, gproj_o, gcoef_o, gstep_o, gcw_o, gcb_o, gsb_o, gdl_o, gsk_o)
    outs_h = (gin_h, ggate_h, gproj_h, gcoef_h, gstep_h, gcw_h, gcb_h, gsb_h, gdl_h, gsk_h)
    z = lax.axis_index("ctx")
    c = lax.axis_index("chan")
    core = lax.rem(c, 2)
    chip = lax.div(c, 2)
    sibling = c + 1 - 2 * core
    nxt = lax.rem(z + 1, Z)
    prv = lax.rem(z + Z - 1, Z)

    def remote(src, dst, send, recv, device):
        return pltpu.make_async_remote_copy(
            src_ref=src, dst_ref=dst, send_sem=send, recv_sem=recv,
            device_id=device, device_id_type=MESH,
        )

    def settle(ref, sem):
        pltpu.make_async_copy(ref, ref, sem).wait()

    def to_ctx(src_of, dst, send, recv):
        @pl.loop(1, Z)
        def _(k):
            peer = lax.rem(z + k, Z)
            remote(src_of(peer), dst, send, recv, {"ctx": peer}).start()

    def lanes(l):
        return slice(LANE * l, LANE * (l + 1))

    def store(i):
        pltpu.make_async_copy(outs_v[i], outs_h[i], osem.at[i]).start()

    pairs = (
        (x_h, x_v), (cw_h, cw_v), (cb_h, cb_v), (pw_h, pw_v), (gate_h, gate_v),
        (og_h, og_v), (sw_h, sw_v), (sb_h, sb_v), (dl_h, dl_v), (sk_h, sk_v),
    )
    loads = [pltpu.make_async_copy(a, b, lsem.at[i]) for i, (a, b) in enumerate(pairs)]
    for load in loads:
        load.start()
    barrier = pltpu.get_barrier_semaphore()

    @pl.loop(1, Z)
    def _(k):
        pl.semaphore_signal(
            barrier, inc=1, device_id={"ctx": lax.rem(z + k, Z)}, device_id_type=MESH
        )

    @pl.loop(1, Q)
    def _(k):
        pl.semaphore_signal(
            barrier, inc=1, device_id={"chan": 2 * lax.rem(chip + k, Q) + core}, device_id_type=MESH
        )

    pl.semaphore_signal(barrier, inc=1, device_id={"chan": sibling}, device_id_type=MESH)
    for load in loads[:4]:
        load.wait()
    pl.semaphore_wait(barrier, Z + Q - 1)

    halo = remote(x_v.at[pl.ds(T - ROWS, ROWS)], halo_v, hs, hr, {"ctx": nxt})
    halo.start()
    xe_v[ROWS:, :] = x_v[...].astype(F32)
    halo.wait_recv()
    xe_v[0:ROWS, :] = jnp.where(z == 0, 0.0, halo_v[...].astype(F32))

    @pl.loop(0, nb)
    def _(b):
        base = pl.multiple_of(b * ROWS, ROWS)
        window = xe_v[pl.ds(base, 2 * ROWS), :]
        pre = jnp.broadcast_to(cb_v[...], (ROWS, C))
        for k in range(K):
            first = ROWS - (K - 1) + k
            pre = pre + cw_v[k : k + 1, :] * window[first : first + ROWS]
        sigma = jax.nn.sigmoid(pre)
        out = (pre * sigma).astype(BF16)
        co_v[pl.ds(base, ROWS), :] = out
        cv_v[pl.ds(base, ROWS), :] = out.astype(F32)
        slope_v[pl.ds(base, ROWS), :] = sigma * (1.0 + pre * (1.0 - sigma))

    half = Q + 1
    mine = core * half
    at_chip = chip + jnp.where(chip > 0, 1, 0)

    def either(when, yes, no):
        pl.when(when)(yes)
        pl.when(jnp.logical_not(when))(no)

    def to_sibling(which):
        remote(
            sbuf.at[pl.ds((1 - core) * half, half)], hbuf,
            send_sums.at[which, 0], recv_sums.at[which, 0], {"chan": sibling},
        ).start()

    def scatter(which):
        settle(hbuf, recv_sums.at[which, 0])
        settle(hbuf, send_sums.at[which, 0])
        both = sbuf[pl.ds(mine, half)].astype(F32) + hbuf[...].astype(F32)
        tbuf[...] = both.astype(BF16)
        send, recv = send_sums.at[which, 1], recv_sums.at[which, 1]

        @pl.loop(1, Q)
        def _(k):
            peer = lax.rem(chip + k, Q)
            device = {"chan": 2 * peer + core}

            def two():
                remote(tbuf.at[pl.ds(0, 2)], rbuf.at[chip], send, recv, device).start()

            def one():
                remote(
                    tbuf.at[pl.ds(peer + 1, 1)], rbuf.at[chip, pl.ds(0, 1)], send, recv, device
                ).start()

            either(peer == 0, two, one)

        rbuf[chip, 0] = tbuf[at_chip]
        rbuf[chip, 1] = tbuf[1]

    def spread(which):
        send, recv = send_sums.at[which, 2], recv_sums.at[which, 2]

        def part(j):
            total = rbuf[0, j].astype(F32)
            for s in range(1, Q):
                total = total + rbuf[s, j].astype(F32)
            return total.astype(BF16)

        def out(block):
            @pl.loop(1, Q)
            def _(k):
                device = {"chan": 2 * lax.rem(chip + k, Q) + core}
                remote(block, block, send, recv, device).start()

        def two():
            settle(rbuf.at[pl.ds(0, Q - 1)], recv_sums.at[which, 1])
            gbuf[mine] = part(0)
            gbuf[mine + 1] = part(1)
            out(gbuf.at[pl.ds(mine, 2)])
            settle(tbuf.at[pl.ds(0, Q - 1)], send_sums.at[which, 1])

        def one():
            settle(rbuf.at[pl.ds(0, Q - 1), pl.ds(0, 1)], recv_sums.at[which, 1])
            gbuf[mine + at_chip] = part(0)
            out(gbuf.at[pl.ds(mine + at_chip, 1)])
            settle(tbuf.at[pl.ds(0, Q)], send_sums.at[which, 1])

        either(chip == 0, two, one)

    def share(which):
        either(
            chip == 0,
            lambda: settle(tbuf.at[pl.ds(0, Q - 1)], recv_sums.at[which, 2]),
            lambda: settle(tbuf.at[pl.ds(0, Q)], recv_sums.at[which, 2]),
        )
        block = gbuf.at[pl.ds(mine, half)]
        remote(
            block, block, send_sums.at[which, 3], recv_sums.at[which, 3], {"chan": sibling}
        ).start()

    def shared(which):
        settle(hbuf, recv_sums.at[which, 3])

    def sums_settle(which):
        either(
            chip == 0,
            lambda: settle(rbuf.at[pl.ds(0, Q - 1)], send_sums.at[which, 2]),
            lambda: settle(rbuf.at[pl.ds(0, Q - 1), pl.ds(0, 1)], send_sums.at[which, 2]),
        )
        settle(hbuf, send_sums.at[which, 3])

    sbuf[...] = dot(pw_v[...], co_v[...], 1, 1).astype(BF16).reshape(Y + 2, ROWS, LANE)
    to_sibling(0)

    for load in loads[4:]:
        load.wait()

    scatter(0)

    @pl.loop(0, nb)
    def _(b):
        rows = pl.ds(pl.multiple_of(b * ROWS, ROWS), ROWS)
        gate = gate_v[rows, :].astype(F32)
        grad = og_v[rows, :].astype(F32)
        sigma = jax.nn.sigmoid(gate)
        g_v[rows, :] = grad * (gate * sigma)
        gg_v[rows, :] = grad * (sigma * (1.0 + gate * (1.0 - sigma)))

    a2 = -jnp.exp(dl_v[...])
    a2_v[...] = a2
    for n in range(N):
        for l in range(CB):
            a3_v[n, l : l + 1, :] = a2[n : n + 1, LANE * l : LANE * (l + 1)] * LOG2E

    spread(0)
    share(0)
    shared(0)
    total = gbuf[...].reshape(R + 2 * N, T)
    slt_v[...] = total[0:R]
    ct_v[...] = total[R:].astype(F32)
    sp_v[...] = dot(total[0:R], sw_v[...], 0, 0)

    def sizes_block(b, carry):
        size_sum, skip_sum = carry
        rows = pl.ds(pl.multiple_of(b * ROWS, ROWS), ROWS)
        pre = sp_v[rows, :] + sb_v[...]
        size = jnp.maximum(pre, 0.0) + jnp.log1p(jnp.exp(-jnp.abs(pre)))
        st_v[rows, :] = size
        sig_v[rows, :] = jax.nn.sigmoid(pre)
        conv = cv_v[rows, :]
        dr_v[rows, :] = size * conv
        size_sum = size_sum + jnp.sum(size, axis=0, keepdims=True)
        skip_sum = skip_sum + jnp.sum(g_v[rows, :] * conv, axis=0, keepdims=True)
        return size_sum, skip_sum

    size_sum, skip_sum = lax.fori_loop(
        0, nb, sizes_block, (jnp.zeros((1, C), F32), jnp.zeros((1, C), F32))
    )
    sums_settle(0)
    oth_v[...] = jnp.zeros_like(oth_v)
    oth_v[K + 2 : K + 3, :] = skip_sum
    for l in range(CB):
        stot_v[z, l : l + 1, :] = size_sum[:, LANE * l : LANE * (l + 1)]
    to_ctx(lambda p: stot_v.at[z], stot_v.at[z], ss_s, ss_r)

    U = 8

    def forward_local(b, h):
        shift = lax.rem(T - b * U, T)
        turned = pltpu.roll(ct_v[...], shift, 1)
        a2s = a2_v[...] * LOG2E
        for i in range(U):
            t = b * U + i
            cols = jnp.broadcast_to(turned[:, i : i + 1], (2 * N, LANE))
            bc_v[t] = cols
            size = st_v[pl.ds(t, 1), :]
            drive = dr_v[pl.ds(t, 1), :]
            f = jnp.exp2(size * a2s)
            f_v[t] = f
            h = f * h + drive * jnp.concatenate([cols[0:N]] * CB, axis=1)
        return h

    end = lax.fori_loop(0, T // U, forward_local, jnp.zeros((N, C), F32))

    def rows_out(values, buf, recv_buf, send, recv):
        for n in range(N):
            p, i = divmod(n, nz)
            for l in range(CB):
                buf[p, i * CB + l : i * CB + l + 1, :] = values[n : n + 1, lanes(l)]
        recv_buf[z] = buf[z]
        to_ctx(lambda p: buf.at[p], recv_buf.at[z], send, recv)

    def rows_combine(recv_buf, out, back, order, recv, send, answer):
        settle(recv_buf.at[pl.ds(0, Z - 1)], recv)
        state = jnp.zeros((nz * CB, LANE), F32)
        for d in order:
            out[d] = state
            state = recv_buf[d] + dec_v[d] * state
        back[z] = out[z]
        to_ctx(lambda p: out.at[p], back.at[z], send, answer)

    def rows_in(back, into, recv):
        settle(back.at[pl.ds(0, Z - 1)], recv)
        for n in range(N):
            p, i = divmod(n, nz)
            for l in range(CB):
                into[n : n + 1, lanes(l)] = back[p, i * CB + l : i * CB + l + 1, :]

    rows_out(end, es_v, er_v, es_s, es_r)

    def backward_local(b, q):
        for i in range(U):
            t = T - 1 - (b * U + i)
            coefs = bc_v[t, N : 2 * N, :]
            q = f_v[t] * (jnp.concatenate([coefs] * CB, axis=1) * g_v[pl.ds(t, 1), :] + q)
        return q

    head = lax.fori_loop(0, T // U, backward_local, jnp.zeros((N, C), F32))
    rows_out(head, hs_v, hr_v, hs_s, hs_r)
    settle(stot_v.at[pl.ds(0, Z - 1)], ss_r)
    for d in range(Z):
        for i in range(nz):
            dec_v[d, i * CB : (i + 1) * CB, :] = jnp.exp2(a3_v[z * nz + i] * stot_v[d])
    rows_combine(er_v, eo_v, ep_v, range(Z), es_r, ep_s, ep_r)
    rows_combine(hr_v, ho_v, hp_v, reversed(range(Z)), hs_r, hp_s, hp_r)
    rows_in(ep_v, sin_v, ep_r)

    lane = lax.broadcasted_iota(jnp.int32, (N, LANE), 1)

    def fold(wide):
        total = wide[:, 0:LANE]
        for l in range(1, CB):
            total = total + wide[:, LANE * l : LANE * (l + 1)]
        return jnp.sum(total, axis=1, keepdims=True)

    def forward_pass(b, carry):
        h, acc = carry
        for i in range(U):
            t = b * U + i
            cols = bc_v[t]
            drive = dr_v[pl.ds(t, 1), :]
            hist_v[t] = h
            h = f_v[t] * h + drive * jnp.concatenate([cols[0:N]] * CB, axis=1)
            out = jnp.concatenate([cols[N : 2 * N]] * CB, axis=1) * h
            so_v[pl.ds(t, 1), :] = jnp.sum(out, axis=0, keepdims=True)
            acc = jnp.where(lane == t, fold(h * g_v[pl.ds(t, 1), :]), acc)
        return h, acc

    _, coef_out = lax.fori_loop(
        0, T // U, forward_pass, (sin_v[...], jnp.zeros((N, LANE), F32))
    )

    rows_in(hp_v, cin_v, hp_r)

    def backward_pass(b, carry):
        q, acc, decay = carry
        a2w = a2_v[...]
        for i in range(U):
            t = T - 1 - (b * U + i)
            cols = bc_v[t]
            g = g_v[pl.ds(t, 1), :]
            adj = jnp.concatenate([cols[N : 2 * N]] * CB, axis=1) * g + q
            q = f_v[t] * adj
            w = q * hist_v[t]
            dd_v[pl.ds(t, 1), :] = jnp.sum(a2w * w, axis=0, keepdims=True)
            ab = jnp.concatenate([cols[0:N]] * CB, axis=1) * adj
            ab_v[pl.ds(t, 1), :] = jnp.sum(ab, axis=0, keepdims=True)
            decay = decay + w * st_v[pl.ds(t, 1), :]
            acc = jnp.where(lane == t, fold(adj * dr_v[pl.ds(t, 1), :]), acc)
        return q, acc, decay

    _, coef_in, decay = lax.fori_loop(
        0, T // U, backward_pass,
        (cin_v[...], jnp.zeros((N, LANE), F32), jnp.zeros((N, C), F32)),
    )
    dg_v[...] = decay * a2_v[...]

    def pre_block(b, bias_sum):
        rows = pl.ds(pl.multiple_of(b * ROWS, ROWS), ROWS)
        pre = (dd_v[rows, :] + ab_v[rows, :] * cv_v[rows, :]) * sig_v[rows, :]
        pre_v[rows, :] = pre.astype(BF16)
        return bias_sum + jnp.sum(pre, axis=0, keepdims=True)

    oth_v[K + 1 : K + 2, :] = lax.fori_loop(0, nb, pre_block, jnp.zeros((1, C), F32))
    back = jnp.concatenate([dot(sw_v[...], pre_v[...], 1, 1), coef_in, coef_out], axis=0)
    sbuf[...] = back.astype(BF16).reshape(Y + 2, ROWS, LANE)
    to_sibling(1)
    gs_v[...] = dot(slt_v[...], pre_v[...], 1, 0).reshape(Z, rz, C)

    def ring(which, part, s):
        left, right = {"ctx": prv}, {"ctx": nxt}
        if s < L:
            value = part[lax.rem(z + Z - L + s, Z)]
            if s:
                settle(lrecv.at[which, s - 1], ls_r.at[which, s - 1])
                value = value + lrecv[which, s - 1].astype(F32)
            lsend[which, s] = value.astype(BF16)
            remote(
                lsend.at[which, s], lrecv.at[which, s],
                ls_s.at[which, s], ls_r.at[which, s], left,
            ).start()
        if s < M:
            value = part[lax.rem(z + M - s, Z)]
            if s:
                settle(mrcv2.at[which, s - 1], ms_r.at[which, s - 1])
                value = value + mrcv2[which, s - 1].astype(F32)
            msend[which, s] = value.astype(BF16)
            remote(
                msend.at[which, s], mrcv2.at[which, s],
                ms_s.at[which, s], ms_r.at[which, s], right,
            ).start()

    def ring_end(which, part):
        value = part[z]
        settle(lrecv.at[which, L - 1], ls_r.at[which, L - 1])
        value = value + lrecv[which, L - 1].astype(F32)
        if M:
            settle(mrcv2.at[which, M - 1], ms_r.at[which, M - 1])
            value = value + mrcv2[which, M - 1].astype(F32)
        for s in range(L):
            settle(lsend.at[which, s], ls_s.at[which, s])
        for s in range(M):
            settle(msend.at[which, s], ms_s.at[which, s])
        return value

    ring(0, gs_v, 0)
    scatter(1)

    @pl.loop(0, nb)
    def _(b):
        rows = pl.ds(pl.multiple_of(b * ROWS, ROWS), ROWS)
        skip = sk_v[...]
        ggate_o[rows, :] = (gg_v[rows, :] * (so_v[rows, :] + skip * cv_v[rows, :])).astype(BF16)
        cg_v[rows, :] = ab_v[rows, :] * st_v[rows, :] + skip * g_v[rows, :]

    store(1)

    other = 8 * CB // Z
    for p in range(Z):
        for i in range(nz):
            for l in range(CB):
                n = p * nz + i
                mf_v[p, i * CB + l : i * CB + l + 1, :] = dg_v[n : n + 1, lanes(l)]
    ring(0, gs_v, 1)
    spread(1)
    ring(0, gs_v, 2)
    share(1)
    ring(0, gs_v, 3)
    shared(1)
    back = gbuf[...].reshape(R + 2 * N, T)
    gp_v[...] = dot(back[0:R], co_v[...], 1, 0).reshape(Z, rz, C)
    ring(1, gp_v, 0)
    sp_v[...] = dot(back, pw_v[...], 0, 0)

    def conv_block(b, carry):
        base = pl.multiple_of(b * ROWS, ROWS)
        rows = pl.ds(base, ROWS)
        grad = (cg_v[rows, :] + sp_v[rows, :]) * slope_v[rows, :]
        dc_v[rows, :] = grad
        window = xe_v[pl.ds(base, 2 * ROWS), :]
        new = []
        for k in range(K):
            first = ROWS - (K - 1) + k
            taps = grad * window[first : first + ROWS]
            new.append(carry[k] + jnp.sum(taps, axis=0, keepdims=True))
        new.append(carry[K] + jnp.sum(grad, axis=0, keepdims=True))
        return tuple(new)

    sums = lax.fori_loop(0, nb, conv_block, (jnp.zeros((1, C), F32),) * (K + 1))
    halo2 = remote(dc_v.at[pl.ds(0, 8)], halo2_v, h2s, h2r, {"ctx": prv})
    halo2.start()
    for k in range(K + 1):
        oth_v[k : k + 1, :] = sums[k]
    gc_v[...] = dot(back[R:], co_v[...], 1, 0)
    for p in range(Z):
        at = nz * CB
        for i in range(other):
            j, l = divmod(p * other + i, CB)
            mf_v[p, at : at + 1, :] = oth_v[j : j + 1, lanes(l)]
            at += 1
        for i in range(coef):
            for l in range(CB):
                n = p * coef + i
                mf_v[p, at : at + 1, :] = gc_v[n : n + 1, lanes(l)]
                at += 1
    mbuf[...] = mf_v[...].astype(BF16)
    mrecv[z] = mbuf[z]
    to_ctx(lambda p: mbuf.at[p], mrecv.at[z], sm_s, sm_r)
    ring(0, gs_v, 4)
    ring(1, gp_v, 1)

    halo2.wait_recv()
    dc_v[pl.ds(T, 8), :] = jnp.where(z == Z - 1, 0.0, halo2_v[...])

    @pl.loop(0, nb)
    def _(b):
        base = pl.multiple_of(b * ROWS, ROWS)
        window = dc_v[pl.ds(base, ROWS + 8), :]
        total = jnp.zeros((ROWS, C), F32)
        for k in range(K):
            lead = K - 1 - k
            total = total + cw_v[k : k + 1, :] * window[lead : lead + ROWS]
        gin_o[pl.ds(base, ROWS), :] = total.astype(BF16)

    store(0)
    ring(0, gs_v, 5)
    ring(1, gp_v, 2)
    settle(mrecv.at[pl.ds(0, Z - 1)], sm_r)
    total = mrecv[0].astype(F32)
    for d in range(1, Z):
        total = total + mrecv[d].astype(F32)
    ag_v[z] = total[0 : ag_v.shape[1]]
    to_ctx(lambda p: ag_v.at[z], ag_v.at[z], sg_s, sg_r)
    for i in range(coef):
        for l in range(CB):
            row = nz * CB + other + i * CB + l
            gcoef_o[i : i + 1, lanes(l)] = total[row : row + 1]
    store(3)
    ring(0, gs_v, 6)
    ring(1, gp_v, 3)
    ring(0, gs_v, 7)
    ring(1, gp_v, 4)
    gstep_o[...] = ring_end(0, gs_v)
    store(4)
    ring(1, gp_v, 5)
    settle(ag_v.at[pl.ds(0, Z - 1)], sg_r)
    outs = [gcw_o.at[k : k + 1] for k in range(K)] + [gcb_o, gsb_o, gsk_o]
    for p in range(Z):
        at = 0
        for i in range(nz):
            for l in range(CB):
                n = p * nz + i
                gdl_o[n : n + 1, lanes(l)] = ag_v[p, at : at + 1, :]
                at += 1
        for i in range(other):
            j, l = divmod(p * other + i, CB)
            if j < len(outs):
                outs[j][:, lanes(l)] = ag_v[p, at : at + 1, :]
            at += 1
    for i in range(5, 10):
        store(i)
    ring(1, gp_v, 6)
    ring(1, gp_v, 7)
    gproj_o[...] = ring_end(1, gp_v)
    store(2)
    halo.wait_send()
    halo2.wait_send()
    sums_settle(1)
    for buf, sem in (
        (stot_v, ss_s), (es_v, es_s), (eo_v, ep_s), (hs_v, hs_s), (ho_v, hp_s), (mbuf, sm_s), (ag_v, sg_s),
    ):
        settle(buf.at[pl.ds(0, Z - 1)], sem)
    for i in range(10):
        pltpu.make_async_copy(outs_v[i], outs_h[i], osem.at[i]).wait()


def hand_on(*refs):
    given, held, result = refs[0:10], refs[20:30], refs[10:20]
    came, went = refs[30:]
    fetch = [pltpu.make_async_copy(a, b, came.at[i]) for i, (a, b) in enumerate(zip(given, held))]
    place = [pltpu.make_async_copy(a, b, went.at[i]) for i, (a, b) in enumerate(zip(held, result))]
    for copy in fetch:
        copy.start()
    for get, put in zip(fetch, place):
        get.wait()
        put.start()
    for copy in place:
        copy.wait()


def body(sizes, *args):
    Z, Y, T, C, R, N, K = sizes
    conv_input, gate, og, cw, cb, pw, sw, sb, dl, sk = args
    CB = C // LANE
    nz = N // Z
    rz = R // Z
    L = Z // 2
    M = max(Z - 1 - L, 1)
    coef = 2 * N // Z
    other = 8 * CB // Z
    er = nz * CB
    small = -(-(er + other + coef * CB) // ROWS) * ROWS
    back = -(-(er + other) // 8) * 8
    half = Y // 2 + 1
    vm = pltpu.VMEM
    dma = pltpu.SemaphoreType.DMA
    scratch = [
        vm((T, C), BF16), vm((T, C), BF16), vm((T, C), BF16), vm((K, C), F32), vm((1, C), F32),
        vm((R + 2 * N, C), BF16), vm((R, C), BF16), vm((1, C), F32), vm((N, C), F32), vm((1, C), F32),
        vm((ROWS, C), BF16), vm((T + ROWS, C), F32), vm((T, C), F32), vm((T, C), BF16), vm((T, C), F32),
        vm((Y + 2, ROWS, LANE), BF16), vm((half, ROWS, LANE), BF16), vm((half, ROWS, LANE), BF16),
        vm((Y // 2, 2, ROWS, LANE), BF16), vm((Y + 2, ROWS, LANE), BF16),
        vm((R, T), BF16), vm((2 * N, T), F32), vm((T, 2 * N, LANE), F32),
        *[vm((T, C), F32) for _ in range(6)],
        vm((Z, CB, LANE), F32), vm((Z, er, LANE), F32), vm((N, C), F32), vm((N, CB, LANE), F32),
        vm((T, N, C), F32), vm((T, N, C), F32),
        *[vm((Z, er, LANE), F32) for _ in range(8)], vm((N, C), F32), vm((N, C), F32),
        vm((T, C), F32), vm((T, C), F32), vm((T, C), F32), vm((T, C), BF16), vm((T, C), F32), vm((N, C), F32),
        vm((Z, rz, C), F32), vm((Z, rz, C), F32), vm((2 * N, C), F32), vm((T + 8, C), F32),
        vm((8, C), F32), vm((8, C), F32),
        vm((Z, small, LANE), F32), vm((Z, small, LANE), BF16), vm((Z, small, LANE), BF16),
        vm((Z, back, LANE), F32),
        vm((2, L, rz, C), BF16), vm((2, L, rz, C), BF16), vm((2, M, rz, C), BF16), vm((2, M, rz, C), BF16),
        dma((10,)), dma((10,)), *[dma(()) for _ in range(18)], dma((2, 4)), dma((2, 4)),
        dma((2, L)), dma((2, L)), dma((2, M)), dma((2, M)),
    ]
    shape = jax.ShapeDtypeStruct
    kinds = [
        shape((T, C), BF16), shape((T, C), BF16), shape((rz, C), F32), shape((coef, C), F32),
        shape((rz, C), F32), shape((K, C), F32), shape((1, C), F32), shape((1, C), F32),
        shape((N, C), F32), shape((1, C), F32),
    ]
    hbm = [pl.BlockSpec(memory_space=pltpu.HBM)] * 10
    outs = pl.pallas_call(
        functools.partial(kernel, sizes),
        out_shape=kinds,
        in_specs=hbm,
        out_specs=hbm,
        scratch_shapes=[vm(k.shape, k.dtype) for k in kinds] + scratch,
        compiler_params=pltpu.CompilerParams(
            collective_id=0, has_side_effects=True, vmem_limit_bytes=VMEM_BYTES
        ),
    )(conv_input, gate, og, cw, cb[None], pw, sw, sb[None], dl, sk[None])
    outs = pl.pallas_call(
        hand_on, out_shape=kinds, in_specs=hbm, out_specs=hbm,
        scratch_shapes=[vm(k.shape, k.dtype) for k in kinds] + [dma((10,)), dma((10,))],
    )(*outs)
    flat = lambda a: a.reshape(-1)
    return (*outs[:6], flat(outs[6]), flat(outs[7]), outs[8], flat(outs[9]))


def solution(mesh):
    Z, Y = mesh.shape["ctx"], mesh.shape["chan"]

    def run(conv_input, *rest):
        cw, pw, sw, dl = rest[2], rest[4], rest[5], rest[7]
        sizes = (
            Z, Y, conv_input.shape[0] // Z, conv_input.shape[1] // Y,
            sw.shape[0], dl.shape[0], cw.shape[0],
        )
        return jax.shard_map(
            functools.partial(body, sizes), mesh=mesh, in_specs=in_specs, out_specs=out_specs,
            check_vma=False,
        )(conv_input, *rest)

    both, wide, flat = P("ctx", "chan"), P(None, "chan"), P("chan")
    in_specs = (both, both, both, wide, flat, wide, wide, flat, wide, flat)
    out_specs = (both, both, both, both, both, wide, flat, flat, wide, flat)
    return run
```

time: 119 us -> 99.7 us (0.84)
  the two profiles are of different devices: /device:TPU:2 before, /device:TPU:32 now
where the time goes in v1:
time: 99.7 us; the launch traced here: 99.5 us
  Pallas kernels  98.9 us (99%)
    pallas_call x1, Pallas kernels, body(): pl.pallas_call(functools.partial(kernel, sizes), out_shape=kinds, in_spec...  97 us

profile of v1, /device:TPU:32, one launch (start us, length us, event | category | flops | bytes accessed | tf_op | source)
XLA Modules:
  0.0 99.5 jit_solution(6310276608883283221)
XLA Ops:
  0.6 97.0 %shard_map.177 = (bf16[128,512]{1,0:T(8,128)(2,1)}, bf16[128,512]{1,0:T(8,128)(2,1)}, f32[32,512]{1,0:T(8,128)}, f32[2,512]{1,0:T(2,128)}, f32[32,512]{1,0:T(8,1...) custom-call(bf16[128,512]{1,0:T(8,128)(2,1)} %refs_0_.1, ...), custom_call_target="tpu_custom_call" | custom-call | tf_op jit(solution)/shard_map/pallas_call | solution.py:623
  97.6 1.9 %shard_map.178 = (bf16[128,512]{1,0:T(8,128)(2,1)}, bf16[128,512]{1,0:T(8,128)(2,1)}, f32[32,512]{1,0:T(8,128)}, f32[2,512]{1,0:T(2,128)}, f32[32,512]{1,0:T(8,1...) custom-call(bf16[128,512]{1,0:T(8,128)(2,1)} %get-tuple-element.30.re, ...), custom_call_target="tpu_custom_call" | custom-call | tf_op jit(solution)/shard_map/pallas_call | solution.py:633

commit v2 on v1

--- a/solution.py
+++ b/solution.py
@@ -16,9 +16,8 @@
 MESH = pl.DeviceIdType.MESH
 
 
-def silu_slope(values):
-    sigma = jax.nn.sigmoid(values)
-    return sigma * (1.0 + values * (1.0 - sigma))
+def group_size(count):
+    return 4 if count % 4 == 0 else count
 
 
 def dot(a, b, over_a, over_b):
@@ -34,6 +33,9 @@
     Q = Y // 2
     coef = 2 * N // Z
     rz = R // Z
+    G = group_size(Z)
+    NG = Z // G
+    rb = rz // ROWS
     L = Z // 2
     M = Z - 1 - L
     nb = T // ROWS
@@ -42,13 +44,14 @@
         gin_h, ggate_h, gproj_h, gcoef_h, gstep_h, gcw_h, gcb_h, gsb_h, gdl_h, gsk_h,
         gin_o, ggate_o, gproj_o, gcoef_o, gstep_o, gcw_o, gcb_o, gsb_o, gdl_o, gsk_o,
         x_v, gate_v, og_v, cw_v, cb_v, pw_v, sw_v, sb_v, dl_v, sk_v,
-        halo_v, xe_v, slope_v, co_v, cv_v, sbuf, hbuf, tbuf, rbuf, gbuf, slt_v, ct_v, bc_v,
+        halo_v, xe_v, slope_v, co_g, cv_v, sbuf, rbuf, gbuf, sl_v, bc_v,
         st_v, sig_v, dr_v, g_v, gg_v, sp_v, stot_v, dec_v, a2_v, a3_v, f_v, hist_v,
         es_v, er_v, eo_v, ep_v, hs_v, hr_v, ho_v, hp_v, sin_v, cin_v,
         so_v, dd_v, ab_v, pre_v, cg_v, dg_v,
-        gs_v, gp_v, gc_v, dc_v, halo2_v, oth_v, mf_v, mbuf, mrecv, ag_v, lsend, lrecv, msend, mrcv2,
+        gs_v, gp_v, bp_g, gc_v, dc_v, halo2_v, oth_v, mf_v, mbuf, mrecv, ag_v,
+        gp_x, gp_y, lsend, lrecv, msend, mrcv2,
         lsem, osem, hs, hr, h2s, h2r, ss_s, ss_r, es_s, es_r, ep_s, ep_r, hs_s, hs_r, hp_s, hp_r,
-        sm_s, sm_r, sg_s, sg_r, send_sums, recv_sums, ls_s, ls_r, ms_s, ms_r,
+        sm_s, sm_r, sg_s, sg_r, send_sums, recv_sums, send_group, recv_group, send_last, recv_last, ls_s, ls_r, ms_s, ms_r,
     ) = refs
     outs_v = (gin_o, ggate_o, gproj_o, gcoef_o, gstep_o, gcw_o, gcb_o, gsb_o, gdl_o, gsk_o)
     outs_h = (gin_h, ggate_h, gproj_h, gcoef_h, gstep_h, gcw_h, gcb_h, gsb_h, gdl_h, gsk_h)
@@ -56,7 +59,8 @@
     c = lax.axis_index("chan")
     core = lax.rem(c, 2)
     chip = lax.div(c, 2)
-    sibling = c + 1 - 2 * core
+    member = lax.rem(z, G)
+    group = lax.div(z, G)
     nxt = lax.rem(z + 1, Z)
     prv = lax.rem(z + Z - 1, Z)
 
@@ -69,10 +73,13 @@
     def settle(ref, sem):
         pltpu.make_async_copy(ref, ref, sem).wait()
 
+    def far_first(j):
+        return L + (j + 1) // 2 * (1 - 2 * (j % 2))
+
     def to_ctx(src_of, dst, send, recv):
-        @pl.loop(1, Z)
-        def _(k):
-            peer = lax.rem(z + k, Z)
+        @pl.loop(0, Z - 1)
+        def _(j):
+            peer = lax.rem(z + far_first(j), Z)
             remote(src_of(peer), dst, send, recv, {"ctx": peer}).start()
 
     def lanes(l):
@@ -90,141 +97,195 @@
         load.start()
     barrier = pltpu.get_barrier_semaphore()
 
+    def greet(device):
+        pl.semaphore_signal(barrier, inc=1, device_id=device, device_id_type=MESH)
+
     @pl.loop(1, Z)
     def _(k):
-        pl.semaphore_signal(
-            barrier, inc=1, device_id={"ctx": lax.rem(z + k, Z)}, device_id_type=MESH
-        )
-
-    @pl.loop(1, Q)
+        greet({"ctx": lax.rem(z + far_first(Z - k - 1), Z)})
+
+    @pl.loop(1, Y)
     def _(k):
-        pl.semaphore_signal(
-            barrier, inc=1, device_id={"chan": 2 * lax.rem(chip + k, Q) + core}, device_id_type=MESH
-        )
-
-    pl.semaphore_signal(barrier, inc=1, device_id={"chan": sibling}, device_id_type=MESH)
-    for load in loads[:4]:
+        greet({"chan": lax.rem(c + k, Y)})
+
+    def conv_rows(b, before):
+        base = pl.multiple_of(b * ROWS, ROWS)
+        rows = pl.ds(base, ROWS)
+        window = jnp.concatenate([before.astype(F32), x_v[rows, :].astype(F32)], axis=0)
+        xe_v[pl.ds(base, 2 * ROWS), :] = window
+        pre = jnp.broadcast_to(cb_v[...], (ROWS, C))
+        for k in range(K):
+            lead = ROWS - (K - 1) + k
+            pre = pre + cw_v[k : k + 1, :] * window[lead : lead + ROWS]
+        sigma = jax.nn.sigmoid(pre)
+        out = (pre * sigma).astype(BF16)
+        co_g[member, rows, :] = out
+        cv_v[rows, :] = out.astype(F32)
+        slope_v[rows, :] = sigma * (1.0 + pre * (1.0 - sigma))
+
+    for load in loads[:3]:
         load.wait()
-    pl.semaphore_wait(barrier, Z + Q - 1)
-
+
+    @pl.loop(1, nb)
+    def _(b):
+        conv_rows(b, x_v[pl.ds(pl.multiple_of((b - 1) * ROWS, ROWS), ROWS), :])
+
+    pl.semaphore_wait(barrier, Z + Y - 2)
     halo = remote(x_v.at[pl.ds(T - ROWS, ROWS)], halo_v, hs, hr, {"ctx": nxt})
     halo.start()
-    xe_v[ROWS:, :] = x_v[...].astype(F32)
+    for load in loads[3:]:
+        load.wait()
+    a2 = -jnp.exp(dl_v[...])
+    a2_v[...] = a2
+    for n in range(N):
+        for l in range(CB):
+            a3_v[n, l : l + 1, :] = a2[n : n + 1, lanes(l)] * LOG2E
     halo.wait_recv()
-    xe_v[0:ROWS, :] = jnp.where(z == 0, 0.0, halo_v[...].astype(F32))
-
-    @pl.loop(0, nb)
-    def _(b):
-        base = pl.multiple_of(b * ROWS, ROWS)
-        window = xe_v[pl.ds(base, 2 * ROWS), :]
-        pre = jnp.broadcast_to(cb_v[...], (ROWS, C))
-        for k in range(K):
-            first = ROWS - (K - 1) + k
-            pre = pre + cw_v[k : k + 1, :] * window[first : first + ROWS]
-        sigma = jax.nn.sigmoid(pre)
-        out = (pre * sigma).astype(BF16)
-        co_v[pl.ds(base, ROWS), :] = out
-        cv_v[pl.ds(base, ROWS), :] = out.astype(F32)
-        slope_v[pl.ds(base, ROWS), :] = sigma * (1.0 + pre * (1.0 - sigma))
-
-    half = Q + 1
-    mine = core * half
-    at_chip = chip + jnp.where(chip > 0, 1, 0)
+    conv_rows(0, jnp.where(z == 0, 0.0, halo_v[...].astype(F32)))
+
+    X = 4 if Q % 4 == 0 and Q > 4 else 2
+    row, col = lax.div(chip, X), lax.rem(chip, X)
+    offsets = sorted(
+        ((dy, dx, dk) for dy in range(Q // X) for dx in range(X) for dk in range(2)),
+        key=lambda o: -min(o[0], Q // X - o[0]) - min(o[1], X - o[1]),
+    )
+    partners = [
+        (lax.rem(row + dy, Q // X) * X + lax.rem(col + dx, X)) * 2 + lax.rem(core + dk, 2)
+        for dy, dx, dk in offsets
+        if dy or dx or dk
+    ]
+
+    def first(d):
+        return d + jnp.where(d > 0, 1, 0) + jnp.where(d > Q, 1, 0)
+
+    def owns_two(d):
+        return jnp.logical_or(d == 0, d == Q)
+
+    mine, double = first(c), owns_two(c)
+    flat_one = rbuf.at[pl.ds(0, Y - 1), pl.ds(0, 1)]
+    flat_two = rbuf.at[pl.ds(0, Y - 1)]
 
     def either(when, yes, no):
         pl.when(when)(yes)
         pl.when(jnp.logical_not(when))(no)
 
-    def to_sibling(which):
-        remote(
-            sbuf.at[pl.ds((1 - core) * half, half)], hbuf,
-            send_sums.at[which, 0], recv_sums.at[which, 0], {"chan": sibling},
-        ).start()
+    def place(p):
+        at = (p % G) * NG * rb + (p // G) * rb
+        return slice(at, at + rb)
+
+    def pack(product, coefs):
+        for p in range(Z):
+            rows = product[rz * p : rz * (p + 1)].astype(BF16)
+            sbuf[place(p)] = rows.reshape(rb, ROWS, LANE)
+        sbuf[Y : Y + 2] = coefs.astype(BF16).reshape(2, ROWS, LANE)
+
+    def unpack():
+        parts = [gbuf[place(p)].reshape(rz, LANE) for p in range(Z)]
+        return jnp.concatenate(parts + [gbuf[Y : Y + 2].reshape(2 * N, LANE)], axis=0)
 
     def scatter(which):
-        settle(hbuf, recv_sums.at[which, 0])
-        settle(hbuf, send_sums.at[which, 0])
-        both = sbuf[pl.ds(mine, half)].astype(F32) + hbuf[...].astype(F32)
-        tbuf[...] = both.astype(BF16)
-        send, recv = send_sums.at[which, 1], recv_sums.at[which, 1]
-
-        @pl.loop(1, Q)
-        def _(k):
-            peer = lax.rem(chip + k, Q)
-            device = {"chan": 2 * peer + core}
+        send, recv = send_sums.at[which, 0], recv_sums.at[which, 0]
+        for d in partners:
+            at = first(d)
 
             def two():
-                remote(tbuf.at[pl.ds(0, 2)], rbuf.at[chip], send, recv, device).start()
+                remote(sbuf.at[pl.ds(at, 2)], rbuf.at[c], send, recv, {"chan": d}).start()
 
             def one():
                 remote(
-                    tbuf.at[pl.ds(peer + 1, 1)], rbuf.at[chip, pl.ds(0, 1)], send, recv, device
+                    sbuf.at[pl.ds(at, 1)], rbuf.at[c, pl.ds(0, 1)], send, recv, {"chan": d}
                 ).start()
 
-            either(peer == 0, two, one)
-
-        rbuf[chip, 0] = tbuf[at_chip]
-        rbuf[chip, 1] = tbuf[1]
+            either(owns_two(d), two, one)
+        rbuf[c, 0] = sbuf[mine]
+        rbuf[c, 1] = sbuf[jnp.minimum(mine + 1, Y + 1)]
 
     def spread(which):
-        send, recv = send_sums.at[which, 2], recv_sums.at[which, 2]
+        send, recv = send_sums.at[which, 1], recv_sums.at[which, 1]
 
         def part(j):
             total = rbuf[0, j].astype(F32)
-            for s in range(1, Q):
+            for s in range(1, Y):
                 total = total + rbuf[s, j].astype(F32)
             return total.astype(BF16)
 
         def out(block):
-            @pl.loop(1, Q)
-            def _(k):
-                device = {"chan": 2 * lax.rem(chip + k, Q) + core}
-                remote(block, block, send, recv, device).start()
+            for d in partners:
+                remote(block, block, send, recv, {"chan": d}).start()
 
         def two():
-            settle(rbuf.at[pl.ds(0, Q - 1)], recv_sums.at[which, 1])
+            settle(flat_two, recv_sums.at[which, 0])
             gbuf[mine] = part(0)
             gbuf[mine + 1] = part(1)
             out(gbuf.at[pl.ds(mine, 2)])
-            settle(tbuf.at[pl.ds(0, Q - 1)], send_sums.at[which, 1])
+            settle(sbuf.at[pl.ds(0, Y)], send_sums.at[which, 0])
 
         def one():
-            settle(rbuf.at[pl.ds(0, Q - 1), pl.ds(0, 1)], recv_sums.at[which, 1])
-            gbuf[mine + at_chip] = part(0)
-            out(gbuf.at[pl.ds(mine + at_chip, 1)])
-            settle(tbuf.at[pl.ds(0, Q)], send_sums.at[which, 1])
-
-        either(chip == 0, two, one)
-
-    def share(which):
+            settle(flat_one, recv_sums.at[which, 0])
+            gbuf[mine] = part(0)
+            out(gbuf.at[pl.ds(mine, 1)])
+            settle(sbuf.at[pl.ds(0, Y + 1)], send_sums.at[which, 0])
+
+        either(double, two, one)
+
+    def shared(which):
         either(
-            chip == 0,
-            lambda: settle(tbuf.at[pl.ds(0, Q - 1)], recv_sums.at[which, 2]),
-            lambda: settle(tbuf.at[pl.ds(0, Q)], recv_sums.at[which, 2]),
+            double,
+            lambda: settle(gbuf.at[pl.ds(0, Y)], recv_sums.at[which, 1]),
+            lambda: settle(gbuf.at[pl.ds(0, Y + 1)], recv_sums.at[which, 1]),
         )
-        block = gbuf.at[pl.ds(mine, half)]
-        remote(
-            block, block, send_sums.at[which, 3], recv_sums.at[which, 3], {"chan": sibling}
-        ).start()
-
-    def shared(which):
-        settle(hbuf, recv_sums.at[which, 3])
 
     def sums_settle(which):
         either(
-            chip == 0,
-            lambda: settle(rbuf.at[pl.ds(0, Q - 1)], send_sums.at[which, 2]),
-            lambda: settle(rbuf.at[pl.ds(0, Q - 1), pl.ds(0, 1)], send_sums.at[which, 2]),
+            double,
+            lambda: settle(flat_two, send_sums.at[which, 1]),
+            lambda: settle(flat_one, send_sums.at[which, 1]),
         )
-        settle(hbuf, send_sums.at[which, 3])
-
-    sbuf[...] = dot(pw_v[...], co_v[...], 1, 1).astype(BF16).reshape(Y + 2, ROWS, LANE)
-    to_sibling(0)
-
-    for load in loads[4:]:
-        load.wait()
-
+
+    def to_group(which, src_of, dst):
+        for k in range(1, G):
+            j = lax.rem(member + k, G)
+            remote(
+                src_of(j), dst, send_group.at[which], recv_group.at[which], {"ctx": group * G + j}
+            ).start()
+
+    def group_ready(which, buf):
+        if G > 1:
+            settle(buf.at[pl.ds(0, G - 1)], recv_group.at[which])
+
+    def group_sent(which, buf):
+        if G > 1:
+            settle(buf.at[pl.ds(0, G - 1)], send_group.at[which])
+
+    def quarter(j):
+        return pl.ds(j * (NG * rb), NG * rb)
+
+    def group_rows(left, right, total, out, back):
+        parts = [left[j].reshape(NG * rz, T) for j in range(G)]
+        product = dot(jnp.concatenate(parts, axis=1), right[...].reshape(G * T, C), 1, 0)
+        total[...] = product.reshape(NG, rz, C)
+        out[...] = product.astype(BF16).reshape(NG, rz, C)
+        for k in range(1, NG):
+            other = lax.rem(group + k, NG)
+            remote(
+                out.at[other], back.at[group], send_last, recv_last,
+                {"ctx": other * G + member},
+            ).start()
+
+    def group_total(total, back):
+        value = total[group]
+        if NG > 1:
+            settle(back.at[pl.ds(0, NG - 1)], recv_last)
+            settle(back.at[pl.ds(0, NG - 1)], send_last)
+        for k in range(1, NG):
+            value = value + back[lax.rem(group + k, NG)].astype(F32)
+        return value
+
+    product = dot(pw_v[...], co_g[member], 1, 1)
+    pack(product[0:R], product[R:])
     scatter(0)
+    to_group(0, lambda j: co_g.at[member], co_g.at[member])
+
 
     @pl.loop(0, nb)
     def _(b):
@@ -235,18 +296,14 @@
         g_v[rows, :] = grad * (gate * sigma)
         gg_v[rows, :] = grad * (sigma * (1.0 + gate * (1.0 - sigma)))
 
-    a2 = -jnp.exp(dl_v[...])
-    a2_v[...] = a2
-    for n in range(N):
-        for l in range(CB):
-            a3_v[n, l : l + 1, :] = a2[n : n + 1, LANE * l : LANE * (l + 1)] * LOG2E
-
     spread(0)
-    share(0)
     shared(0)
-    total = gbuf[...].reshape(R + 2 * N, T)
-    slt_v[...] = total[0:R]
-    ct_v[...] = total[R:].astype(F32)
+
+    total = unpack()
+    sl_v[...] = gbuf[0:Y].reshape(R, T)
+    coefs = total[R:].astype(F32)
+    for t in range(T):
+        bc_v[t] = jnp.broadcast_to(coefs[:, t : t + 1], (2 * N, LANE))
     sp_v[...] = dot(total[0:R], sw_v[...], 0, 0)
 
     def sizes_block(b, carry):
@@ -275,18 +332,15 @@
     U = 8
 
     def forward_local(b, h):
-        shift = lax.rem(T - b * U, T)
-        turned = pltpu.roll(ct_v[...], shift, 1)
         a2s = a2_v[...] * LOG2E
         for i in range(U):
             t = b * U + i
-            cols = jnp.broadcast_to(turned[:, i : i + 1], (2 * N, LANE))
-            bc_v[t] = cols
+            cols = bc_v[t, 0:N, :]
             size = st_v[pl.ds(t, 1), :]
             drive = dr_v[pl.ds(t, 1), :]
             f = jnp.exp2(size * a2s)
             f_v[t] = f
-            h = f * h + drive * jnp.concatenate([cols[0:N]] * CB, axis=1)
+            h = f * h + drive * jnp.concatenate([cols] * CB, axis=1)
         return h
 
     end = lax.fori_loop(0, T // U, forward_local, jnp.zeros((N, C), F32))
@@ -391,49 +445,50 @@
         return bias_sum + jnp.sum(pre, axis=0, keepdims=True)
 
     oth_v[K + 1 : K + 2, :] = lax.fori_loop(0, nb, pre_block, jnp.zeros((1, C), F32))
-    back = jnp.concatenate([dot(sw_v[...], pre_v[...], 1, 1), coef_in, coef_out], axis=0)
-    sbuf[...] = back.astype(BF16).reshape(Y + 2, ROWS, LANE)
-    to_sibling(1)
-    gs_v[...] = dot(slt_v[...], pre_v[...], 1, 0).reshape(Z, rz, C)
-
-    def ring(which, part, s):
+    pack(dot(sw_v[...], pre_v[...], 1, 1), jnp.concatenate([coef_in, coef_out], axis=0))
+    scatter(1)
+    gs_v[...] = dot(sl_v[...], pre_v[...], 1, 0).reshape(Z, rz, C)
+
+    def piece(p):
+        return lax.rem(p, G) * NG + lax.div(p, G)
+
+    def ring(s):
         left, right = {"ctx": prv}, {"ctx": nxt}
         if s < L:
-            value = part[lax.rem(z + Z - L + s, Z)]
+            value = gs_v[piece(lax.rem(z + Z - L + s, Z))]
             if s:
-                settle(lrecv.at[which, s - 1], ls_r.at[which, s - 1])
-                value = value + lrecv[which, s - 1].astype(F32)
-            lsend[which, s] = value.astype(BF16)
+                settle(lrecv.at[s - 1], ls_r.at[s - 1])
+                value = value + lrecv[s - 1].astype(F32)
+            lsend[s] = value.astype(BF16)
             remote(
-                lsend.at[which, s], lrecv.at[which, s],
-                ls_s.at[which, s], ls_r.at[which, s], left,
+                lsend.at[s], lrecv.at[s],
+                ls_s.at[s], ls_r.at[s], left,
             ).start()
         if s < M:
-            value = part[lax.rem(z + M - s, Z)]
+            value = gs_v[piece(lax.rem(z + M - s, Z))]
             if s:
-                settle(mrcv2.at[which, s - 1], ms_r.at[which, s - 1])
-                value = value + mrcv2[which, s - 1].astype(F32)
-            msend[which, s] = value.astype(BF16)
+                settle(mrcv2.at[s - 1], ms_r.at[s - 1])
+                value = value + mrcv2[s - 1].astype(F32)
+            msend[s] = value.astype(BF16)
             remote(
-                msend.at[which, s], mrcv2.at[which, s],
-                ms_s.at[which, s], ms_r.at[which, s], right,
+                msend.at[s], mrcv2.at[s],
+                ms_s.at[s], ms_r.at[s], right,
             ).start()
 
-    def ring_end(which, part):
-        value = part[z]
-        settle(lrecv.at[which, L - 1], ls_r.at[which, L - 1])
-        value = value + lrecv[which, L - 1].astype(F32)
+    def ring_end():
+        value = gs_v[piece(z)]
+        settle(lrecv.at[L - 1], ls_r.at[L - 1])
+        value = value + lrecv[L - 1].astype(F32)
         if M:
-            settle(mrcv2.at[which, M - 1], ms_r.at[which, M - 1])
-            value = value + mrcv2[which, M - 1].astype(F32)
+            settle(mrcv2.at[M - 1], ms_r.at[M - 1])
+            value = value + mrcv2[M - 1].astype(F32)
         for s in range(L):
-            settle(lsend.at[which, s], ls_s.at[which, s])
+            settle(lsend.at[s], ls_s.at[s])
         for s in range(M):
-            settle(msend.at[which, s], ms_s.at[which, s])
+            settle(msend.at[s], ms_s.at[s])
         return value
 
-    ring(0, gs_v, 0)
-    scatter(1)
+    ring(0)
 
     @pl.loop(0, nb)
     def _(b):
@@ -450,16 +505,15 @@
             for l in range(CB):
                 n = p * nz + i
                 mf_v[p, i * CB + l : i * CB + l + 1, :] = dg_v[n : n + 1, lanes(l)]
-    ring(0, gs_v, 1)
+    ring(1)
     spread(1)
-    ring(0, gs_v, 2)
-    share(1)
-    ring(0, gs_v, 3)
+    ring(2)
     shared(1)
-    back = gbuf[...].reshape(R + 2 * N, T)
-    gp_v[...] = dot(back[0:R], co_v[...], 1, 0).reshape(Z, rz, C)
-    ring(1, gp_v, 0)
+    bp_g[member] = gbuf[quarter(member)]
+    to_group(1, lambda j: gbuf.at[quarter(j)], bp_g.at[member])
+    back = unpack()
     sp_v[...] = dot(back, pw_v[...], 0, 0)
+    ring(3)
 
     def conv_block(b, carry):
         base = pl.multiple_of(b * ROWS, ROWS)
@@ -480,7 +534,7 @@
     halo2.start()
     for k in range(K + 1):
         oth_v[k : k + 1, :] = sums[k]
-    gc_v[...] = dot(back[R:], co_v[...], 1, 0)
+    gc_v[...] = dot(back[R:], co_g[member], 1, 0)
     for p in range(Z):
         at = nz * CB
         for i in range(other):
@@ -495,8 +549,11 @@
     mbuf[...] = mf_v[...].astype(BF16)
     mrecv[z] = mbuf[z]
     to_ctx(lambda p: mbuf.at[p], mrecv.at[z], sm_s, sm_r)
-    ring(0, gs_v, 4)
-    ring(1, gp_v, 1)
+    ring(4)
+    group_ready(0, co_g)
+    group_ready(1, bp_g)
+    group_rows(bp_g, co_g, gp_v, gp_x, gp_y)
+    ring(5)
 
     halo2.wait_recv()
     dc_v[pl.ds(T, 8), :] = jnp.where(z == Z - 1, 0.0, halo2_v[...])
@@ -512,8 +569,7 @@
         gin_o[pl.ds(base, ROWS), :] = total.astype(BF16)
 
     store(0)
-    ring(0, gs_v, 5)
-    ring(1, gp_v, 2)
+    ring(6)
     settle(mrecv.at[pl.ds(0, Z - 1)], sm_r)
     total = mrecv[0].astype(F32)
     for d in range(1, Z):
@@ -525,13 +581,9 @@
             row = nz * CB + other + i * CB + l
             gcoef_o[i : i + 1, lanes(l)] = total[row : row + 1]
     store(3)
-    ring(0, gs_v, 6)
-    ring(1, gp_v, 3)
-    ring(0, gs_v, 7)
-    ring(1, gp_v, 4)
-    gstep_o[...] = ring_end(0, gs_v)
+    ring(7)
+    gstep_o[...] = ring_end()
     store(4)
-    ring(1, gp_v, 5)
     settle(ag_v.at[pl.ds(0, Z - 1)], sg_r)
     outs = [gcw_o.at[k : k + 1] for k in range(K)] + [gcb_o, gsb_o, gsk_o]
     for p in range(Z):
@@ -548,10 +600,10 @@
             at += 1
     for i in range(5, 10):
         store(i)
-    ring(1, gp_v, 6)
-    ring(1, gp_v, 7)
-    gproj_o[...] = ring_end(1, gp_v)
+    gproj_o[...] = group_total(gp_v, gp_y)
     store(2)
+    for which, buf in ((0, co_g), (1, bp_g)):
+        group_sent(which, buf)
     halo.wait_send()
     halo2.wait_send()
     sums_settle(1)
@@ -590,28 +642,31 @@
     er = nz * CB
     small = -(-(er + other + coef * CB) // ROWS) * ROWS
     back = -(-(er + other) // 8) * 8
-    half = Y // 2 + 1
+    G = group_size(Z)
+    NG = Z // G
+    rb = rz // ROWS
     vm = pltpu.VMEM
     dma = pltpu.SemaphoreType.DMA
     scratch = [
         vm((T, C), BF16), vm((T, C), BF16), vm((T, C), BF16), vm((K, C), F32), vm((1, C), F32),
         vm((R + 2 * N, C), BF16), vm((R, C), BF16), vm((1, C), F32), vm((N, C), F32), vm((1, C), F32),
-        vm((ROWS, C), BF16), vm((T + ROWS, C), F32), vm((T, C), F32), vm((T, C), BF16), vm((T, C), F32),
-        vm((Y + 2, ROWS, LANE), BF16), vm((half, ROWS, LANE), BF16), vm((half, ROWS, LANE), BF16),
-        vm((Y // 2, 2, ROWS, LANE), BF16), vm((Y + 2, ROWS, LANE), BF16),
-        vm((R, T), BF16), vm((2 * N, T), F32), vm((T, 2 * N, LANE), F32),
+        vm((ROWS, C), BF16), vm((T + ROWS, C), F32), vm((T, C), F32), vm((G, T, C), BF16), vm((T, C), F32),
+        vm((Y + 2, ROWS, LANE), BF16), vm((Y, 2, ROWS, LANE), BF16), vm((Y + 2, ROWS, LANE), BF16),
+        vm((R, T), BF16), vm((T, 2 * N, LANE), F32),
         *[vm((T, C), F32) for _ in range(6)],
         vm((Z, CB, LANE), F32), vm((Z, er, LANE), F32), vm((N, C), F32), vm((N, CB, LANE), F32),
         vm((T, N, C), F32), vm((T, N, C), F32),
         *[vm((Z, er, LANE), F32) for _ in range(8)], vm((N, C), F32), vm((N, C), F32),
         vm((T, C), F32), vm((T, C), F32), vm((T, C), F32), vm((T, C), BF16), vm((T, C), F32), vm((N, C), F32),
-        vm((Z, rz, C), F32), vm((Z, rz, C), F32), vm((2 * N, C), F32), vm((T + 8, C), F32),
+        vm((Z, rz, C), F32), vm((NG, rz, C), F32), vm((G, NG * rb, ROWS, T), BF16), vm((2 * N, C), F32),
+        vm((T + 8, C), F32),
         vm((8, C), F32), vm((8, C), F32),
         vm((Z, small, LANE), F32), vm((Z, small, LANE), BF16), vm((Z, small, LANE), BF16),
         vm((Z, back, LANE), F32),
-        vm((2, L, rz, C), BF16), vm((2, L, rz, C), BF16), vm((2, M, rz, C), BF16), vm((2, M, rz, C), BF16),
-        dma((10,)), dma((10,)), *[dma(()) for _ in range(18)], dma((2, 4)), dma((2, 4)),
-        dma((2, L)), dma((2, L)), dma((2, M)), dma((2, M)),
+        vm((NG, rz, C), BF16), vm((NG, rz, C), BF16),
+        vm((L, rz, C), BF16), vm((L, rz, C), BF16), vm((M, rz, C), BF16), vm((M, rz, C), BF16),
+        dma((10,)), dma((10,)), *[dma(()) for _ in range(18)], dma((2, 2)), dma((2, 2)),
+        dma((2,)), dma((2,)), dma(()), dma(()), dma((L,)), dma((L,)), dma((M,)), dma((M,)),
     ]
     shape = jax.ShapeDtypeStruct
     kinds = [

time: 99.7 us -> 89.7 us (0.90)
  the two profiles are of different devices: /device:TPU:32 before, /device:TPU:2 now
where the time goes in v2:
time: 89.7 us; the launch traced here: 89.5 us
  Pallas kernels  88.9 us (99%)
    pallas_call x1, Pallas kernels, body(): pl.pallas_call(functools.partial(kernel, sizes), out_shape=kinds, in_spec...  87 us
    pallas_call x1, Pallas kernels, body(): pl.pallas_call(hand_on, out_shape=kinds, in_specs=hbm, out_specs=hbm, scr...  1.87 us

profile of v2, /device:TPU:2, one launch (start us, length us, event | category | flops | bytes accessed | tf_op | source)
XLA Modules:
  0.0 89.5 jit_solution(1870543111486861407)
XLA Ops:
  0.6 87.0 %shard_map.177 = (bf16[128,512]{1,0:T(8,128)(2,1)}, bf16[128,512]{1,0:T(8,128)(2,1)}, f32[32,512]{1,0:T(8,128)}, f32[2,512]{1,0:T(2,128)}, f32[32,512]{1,0:T(8,1...) custom-call(bf16[128,512]{1,0:T(8,128)(2,1)} %refs_0_.1, ...), custom_call_target="tpu_custom_call" | custom-call | tf_op jit(solution)/shard_map/pallas_call | solution.py:678
  87.7 1.9 %shard_map.178 = (bf16[128,512]{1,0:T(8,128)(2,1)}, bf16[128,512]{1,0:T(8,128)(2,1)}, f32[32,512]{1,0:T(8,128)}, f32[2,512]{1,0:T(2,128)}, f32[32,512]{1,0:T(8,1...) custom-call(bf16[128,512]{1,0:T(8,128)(2,1)} %get-tuple-element.30.re, ...), custom_call_target="tpu_custom_call" | custom-call | tf_op jit(solution)/shard_map/pallas_call | solution.py:688

commit v3 on v2

--- a/solution.py
+++ b/solution.py
@@ -45,12 +45,12 @@
         gin_o, ggate_o, gproj_o, gcoef_o, gstep_o, gcw_o, gcb_o, gsb_o, gdl_o, gsk_o,
         x_v, gate_v, og_v, cw_v, cb_v, pw_v, sw_v, sb_v, dl_v, sk_v,
         halo_v, xe_v, slope_v, co_g, cv_v, sbuf, rbuf, gbuf, sl_v, bc_v,
-        st_v, sig_v, dr_v, g_v, gg_v, sp_v, stot_v, dec_v, a2_v, a3_v, f_v, hist_v,
+        st_v, sig_v, dr_v, g_v, gg_v, sp_v, dec_v, a2_v, a3_v, f_v, hist_v,
         es_v, er_v, eo_v, ep_v, hs_v, hr_v, ho_v, hp_v, sin_v, cin_v,
         so_v, dd_v, ab_v, pre_v, cg_v, dg_v,
-        gs_v, gp_v, bp_g, gc_v, dc_v, halo2_v, oth_v, mf_v, mbuf, mrecv, ag_v,
+        gs_v, gp_v, bp_g, gc_v, dc_v, halo2_v, oth_v, few_v, kf_v, kr_v, ka_v, mf_v, mbuf, mrecv, ag_v,
         gp_x, gp_y, lsend, lrecv, msend, mrcv2,
-        lsem, osem, hs, hr, h2s, h2r, ss_s, ss_r, es_s, es_r, ep_s, ep_r, hs_s, hs_r, hp_s, hp_r,
+        lsem, osem, hs, hr, h2s, h2r, kk_s, kk_r, ka_s, ka_r, es_s, es_r, ep_s, ep_r, hs_s, hs_r, hp_s, hp_r,
         sm_s, sm_r, sg_s, sg_r, send_sums, recv_sums, send_group, recv_group, send_last, recv_last, ls_s, ls_r, ms_s, ms_r,
     ) = refs
     outs_v = (gin_o, ggate_o, gproj_o, gcoef_o, gstep_o, gcw_o, gcb_o, gsb_o, gdl_o, gsk_o)
@@ -324,12 +324,9 @@
     )
     sums_settle(0)
     oth_v[...] = jnp.zeros_like(oth_v)
-    oth_v[K + 2 : K + 3, :] = skip_sum
-    for l in range(CB):
-        stot_v[z, l : l + 1, :] = size_sum[:, LANE * l : LANE * (l + 1)]
-    to_ctx(lambda p: stot_v.at[z], stot_v.at[z], ss_s, ss_r)
-
-    U = 8
+    few_v[...] = jnp.zeros_like(few_v)
+    few_v[1:2, :] = skip_sum
+    U = 32
 
     def forward_local(b, h):
         a2s = a2_v[...] * LOG2E
@@ -345,20 +342,25 @@
 
     end = lax.fori_loop(0, T // U, forward_local, jnp.zeros((N, C), F32))
 
-    def rows_out(values, buf, recv_buf, send, recv):
+    def rows_out(values, buf, recv_buf, send, recv, extra=None):
         for n in range(N):
             p, i = divmod(n, nz)
             for l in range(CB):
                 buf[p, i * CB + l : i * CB + l + 1, :] = values[n : n + 1, lanes(l)]
+        if extra is not None:
+            for l in range(CB):
+                row = jnp.broadcast_to(extra[:, lanes(l)].reshape(1, 1, LANE), (Z, 1, LANE))
+                buf[:, nz * CB + l : nz * CB + l + 1, :] = row
         recv_buf[z] = buf[z]
         to_ctx(lambda p: buf.at[p], recv_buf.at[z], send, recv)
 
     def rows_combine(recv_buf, out, back, order, recv, send, answer):
-        settle(recv_buf.at[pl.ds(0, Z - 1)], recv)
+        if recv is not None:
+            settle(recv_buf.at[pl.ds(0, Z - 1)], recv)
         state = jnp.zeros((nz * CB, LANE), F32)
         for d in order:
             out[d] = state
-            state = recv_buf[d] + dec_v[d] * state
+            state = recv_buf[d, 0 : nz * CB, :] + dec_v[d] * state
         back[z] = out[z]
         to_ctx(lambda p: out.at[p], back.at[z], send, answer)
 
@@ -369,7 +371,7 @@
             for l in range(CB):
                 into[n : n + 1, lanes(l)] = back[p, i * CB + l : i * CB + l + 1, :]
 
-    rows_out(end, es_v, er_v, es_s, es_r)
+    rows_out(end, es_v, er_v, es_s, es_r, size_sum)
 
     def backward_local(b, q):
         for i in range(U):
@@ -380,11 +382,12 @@
 
     head = lax.fori_loop(0, T // U, backward_local, jnp.zeros((N, C), F32))
     rows_out(head, hs_v, hr_v, hs_s, hs_r)
-    settle(stot_v.at[pl.ds(0, Z - 1)], ss_r)
+    settle(er_v.at[pl.ds(0, Z - 1)], es_r)
     for d in range(Z):
         for i in range(nz):
-            dec_v[d, i * CB : (i + 1) * CB, :] = jnp.exp2(a3_v[z * nz + i] * stot_v[d])
-    rows_combine(er_v, eo_v, ep_v, range(Z), es_r, ep_s, ep_r)
+            total_size = er_v[d, nz * CB : (nz + 1) * CB, :]
+            dec_v[d, i * CB : (i + 1) * CB, :] = jnp.exp2(a3_v[z * nz + i] * total_size)
+    rows_combine(er_v, eo_v, ep_v, range(Z), None, ep_s, ep_r)
     rows_combine(hr_v, ho_v, hp_v, reversed(range(Z)), hs_r, hp_s, hp_r)
     rows_in(ep_v, sin_v, ep_r)
 
@@ -444,7 +447,7 @@
         pre_v[rows, :] = pre.astype(BF16)
         return bias_sum + jnp.sum(pre, axis=0, keepdims=True)
 
-    oth_v[K + 1 : K + 2, :] = lax.fori_loop(0, nb, pre_block, jnp.zeros((1, C), F32))
+    few_v[0:1, :] = lax.fori_loop(0, nb, pre_block, jnp.zeros((1, C), F32))
     pack(dot(sw_v[...], pre_v[...], 1, 1), jnp.concatenate([coef_in, coef_out], axis=0))
     scatter(1)
     gs_v[...] = dot(sl_v[...], pre_v[...], 1, 0).reshape(Z, rz, C)
@@ -499,21 +502,38 @@
 
     store(1)
 
-    other = 8 * CB // Z
+    def rows_of(p, source, count):
+        for i in range(count):
+            n, l = divmod(p * count + i, CB)
+            yield i, source, n, l
+
+    def sum_rows(buf, recv_buf, back_buf, recv, send, answer, rows):
+        settle(recv_buf.at[pl.ds(0, Z - 1)], recv)
+        total = recv_buf[0].astype(F32)
+        for d in range(1, Z):
+            total = total + recv_buf[d].astype(F32)
+        back_buf[z] = total[0:rows]
+        to_ctx(lambda p: back_buf.at[z], back_buf.at[z], send, answer)
+        return total
+
+    few = 4 * CB // Z
     for p in range(Z):
-        for i in range(nz):
-            for l in range(CB):
-                n = p * nz + i
-                mf_v[p, i * CB + l : i * CB + l + 1, :] = dg_v[n : n + 1, lanes(l)]
+        for i, ref, n, l in rows_of(p, dg_v, nz * CB):
+            kf_v[p, i : i + 1, :] = ref[n : n + 1, lanes(l)]
+        for i, ref, n, l in rows_of(p, few_v, few):
+            kf_v[p, nz * CB + i : nz * CB + i + 1, :] = ref[n : n + 1, lanes(l)]
+    kr_v[z] = kf_v[z]
+    to_ctx(lambda p: kf_v.at[p], kr_v.at[z], kk_s, kk_r)
     ring(1)
     spread(1)
     ring(2)
+    sum_rows(kf_v, kr_v, ka_v, kk_r, ka_s, ka_r, nz * CB + few)
     shared(1)
+    ring(3)
     bp_g[member] = gbuf[quarter(member)]
     to_group(1, lambda j: gbuf.at[quarter(j)], bp_g.at[member])
     back = unpack()
     sp_v[...] = dot(back, pw_v[...], 0, 0)
-    ring(3)
 
     def conv_block(b, carry):
         base = pl.multiple_of(b * ROWS, ROWS)
@@ -535,17 +555,12 @@
     for k in range(K + 1):
         oth_v[k : k + 1, :] = sums[k]
     gc_v[...] = dot(back[R:], co_g[member], 1, 0)
+    other = 8 * CB // Z
     for p in range(Z):
-        at = nz * CB
-        for i in range(other):
-            j, l = divmod(p * other + i, CB)
-            mf_v[p, at : at + 1, :] = oth_v[j : j + 1, lanes(l)]
-            at += 1
-        for i in range(coef):
-            for l in range(CB):
-                n = p * coef + i
-                mf_v[p, at : at + 1, :] = gc_v[n : n + 1, lanes(l)]
-                at += 1
+        for i, ref, n, l in rows_of(p, oth_v, other):
+            mf_v[p, i : i + 1, :] = ref[n : n + 1, lanes(l)]
+        for i, ref, n, l in rows_of(p, gc_v, coef * CB):
+            mf_v[p, other + i : other + i + 1, :] = ref[n : n + 1, lanes(l)]
     mbuf[...] = mf_v[...].astype(BF16)
     mrecv[z] = mbuf[z]
     to_ctx(lambda p: mbuf.at[p], mrecv.at[z], sm_s, sm_r)
@@ -569,36 +584,33 @@
         gin_o[pl.ds(base, ROWS), :] = total.astype(BF16)
 
     store(0)
-    ring(6)
-    settle(mrecv.at[pl.ds(0, Z - 1)], sm_r)
-    total = mrecv[0].astype(F32)
-    for d in range(1, Z):
-        total = total + mrecv[d].astype(F32)
-    ag_v[z] = total[0 : ag_v.shape[1]]
-    to_ctx(lambda p: ag_v.at[z], ag_v.at[z], sg_s, sg_r)
+    total = sum_rows(mbuf, mrecv, ag_v, sm_r, sg_s, sg_r, other)
     for i in range(coef):
         for l in range(CB):
-            row = nz * CB + other + i * CB + l
-            gcoef_o[i : i + 1, lanes(l)] = total[row : row + 1]
+            at = other + i * CB + l
+            gcoef_o[i : i + 1, lanes(l)] = total[at : at + 1]
     store(3)
+    ring(6)
     ring(7)
+    settle(ka_v.at[pl.ds(0, Z - 1)], ka_r)
+    for p in range(Z):
+        for i, ref, n, l in rows_of(p, gdl_o, nz * CB):
+            ref[n : n + 1, lanes(l)] = ka_v[p, i : i + 1, :]
+        for i, _, n, l in rows_of(p, None, few):
+            if n < 2:
+                (gsb_o, gsk_o)[n][:, lanes(l)] = ka_v[p, nz * CB + i : nz * CB + i + 1, :]
+    for i in (7, 8, 9):
+        store(i)
     gstep_o[...] = ring_end()
     store(4)
     settle(ag_v.at[pl.ds(0, Z - 1)], sg_r)
-    outs = [gcw_o.at[k : k + 1] for k in range(K)] + [gcb_o, gsb_o, gsk_o]
     for p in range(Z):
-        at = 0
-        for i in range(nz):
-            for l in range(CB):
-                n = p * nz + i
-                gdl_o[n : n + 1, lanes(l)] = ag_v[p, at : at + 1, :]
-                at += 1
-        for i in range(other):
-            j, l = divmod(p * other + i, CB)
-            if j < len(outs):
-                outs[j][:, lanes(l)] = ag_v[p, at : at + 1, :]
-            at += 1
-    for i in range(5, 10):
+        for i, _, n, l in rows_of(p, None, other):
+            if n < K:
+                gcw_o[n : n + 1, lanes(l)] = ag_v[p, i : i + 1, :]
+            elif n == K:
+                gcb_o[:, lanes(l)] = ag_v[p, i : i + 1, :]
+    for i in (5, 6):
         store(i)
     gproj_o[...] = group_total(gp_v, gp_y)
     store(2)
@@ -608,7 +620,7 @@
     halo2.wait_send()
     sums_settle(1)
     for buf, sem in (
-        (stot_v, ss_s), (es_v, es_s), (eo_v, ep_s), (hs_v, hs_s), (ho_v, hp_s), (mbuf, sm_s), (ag_v, sg_s),
+        (es_v, es_s), (eo_v, ep_s), (hs_v, hs_s), (ho_v, hp_s), (mbuf, sm_s), (ag_v, sg_s), (kf_v, kk_s), (ka_v, ka_s),
     ):
         settle(buf.at[pl.ds(0, Z - 1)], sem)
     for i in range(10):
@@ -640,8 +652,9 @@
     coef = 2 * N // Z
     other = 8 * CB // Z
     er = nz * CB
-    small = -(-(er + other + coef * CB) // ROWS) * ROWS
-    back = -(-(er + other) // 8) * 8
+    few = 4 * CB // Z
+    kept = -(-(er + few) // 8) * 8
+    small = -(-(other + coef * CB) // ROWS) * ROWS
     G = group_size(Z)
     NG = Z // G
     rb = rz // ROWS
@@ -654,18 +667,20 @@
         vm((Y + 2, ROWS, LANE), BF16), vm((Y, 2, ROWS, LANE), BF16), vm((Y + 2, ROWS, LANE), BF16),
         vm((R, T), BF16), vm((T, 2 * N, LANE), F32),
         *[vm((T, C), F32) for _ in range(6)],
-        vm((Z, CB, LANE), F32), vm((Z, er, LANE), F32), vm((N, C), F32), vm((N, CB, LANE), F32),
+        vm((Z, er, LANE), F32), vm((N, C), F32), vm((N, CB, LANE), F32),
         vm((T, N, C), F32), vm((T, N, C), F32),
-        *[vm((Z, er, LANE), F32) for _ in range(8)], vm((N, C), F32), vm((N, C), F32),
+        *[vm((Z, er + CB, LANE), F32) for _ in range(2)], *[vm((Z, er, LANE), F32) for _ in range(6)],
+        vm((N, C), F32), vm((N, C), F32),
         vm((T, C), F32), vm((T, C), F32), vm((T, C), F32), vm((T, C), BF16), vm((T, C), F32), vm((N, C), F32),
         vm((Z, rz, C), F32), vm((NG, rz, C), F32), vm((G, NG * rb, ROWS, T), BF16), vm((2 * N, C), F32),
         vm((T + 8, C), F32),
-        vm((8, C), F32), vm((8, C), F32),
+        vm((8, C), F32), vm((8, C), F32), vm((4, C), F32),
+        vm((Z, kept, LANE), F32), vm((Z, kept, LANE), F32), vm((Z, er + few, LANE), F32),
         vm((Z, small, LANE), F32), vm((Z, small, LANE), BF16), vm((Z, small, LANE), BF16),
-        vm((Z, back, LANE), F32),
+        vm((Z, other, LANE), F32),
         vm((NG, rz, C), BF16), vm((NG, rz, C), BF16),
         vm((L, rz, C), BF16), vm((L, rz, C), BF16), vm((M, rz, C), BF16), vm((M, rz, C), BF16),
-        dma((10,)), dma((10,)), *[dma(()) for _ in range(18)], dma((2, 2)), dma((2, 2)),
+        dma((10,)), dma((10,)), *[dma(()) for _ in range(20)], dma((2, 2)), dma((2, 2)),
         dma((2,)), dma((2,)), dma(()), dma(()), dma((L,)), dma((L,)), dma((M,)), dma((M,)),
     ]
     shape = jax.ShapeDtypeStruct

time: 89.7 us -> 87.1 us (0.971)
  Pallas kernels: 88.9 us -> 86.3 us
    pallas_call x1, Pallas kernels: 87 us -> 84.5 us  [body(): pl.pallas_call(functools.partial(kernel, sizes), out_shape=kinds, in_spec...]
where the time goes in v3:
time: 87.1 us; the launch traced here: 87 us
  Pallas kernels  86.3 us (99%)
    pallas_call x1, Pallas kernels, body(): pl.pallas_call(functools.partial(kernel, sizes), out_shape=kinds, in_spec...  84.5 us
    pallas_call x1, Pallas kernels, body(): pl.pallas_call(hand_on, out_shape=kinds, in_specs=hbm, out_specs=hbm, scr...  1.87 us

profile of v3, /device:TPU:2, one launch (start us, length us, event | category | flops | bytes accessed | tf_op | source)
XLA Modules:
  0.0 87.0 jit_solution(4936876325571695636)
XLA Ops:
  0.6 84.5 %shard_map.177 = (bf16[128,512]{1,0:T(8,128)(2,1)}, bf16[128,512]{1,0:T(8,128)(2,1)}, f32[32,512]{1,0:T(8,128)}, f32[2,512]{1,0:T(2,128)}, f32[32,512]{1,0:T(8,1...) custom-call(bf16[128,512]{1,0:T(8,128)(2,1)} %refs_0_.1, ...), custom_call_target="tpu_custom_call" | custom-call | tf_op jit(solution)/shard_map/pallas_call | solution.py:693
  85.1 1.9 %shard_map.178 = (bf16[128,512]{1,0:T(8,128)(2,1)}, bf16[128,512]{1,0:T(8,128)(2,1)}, f32[32,512]{1,0:T(8,128)}, f32[2,512]{1,0:T(2,128)}, f32[32,512]{1,0:T(8,1...) custom-call(bf16[128,512]{1,0:T(8,128)(2,1)} %get-tuple-element.30.re, ...), custom_call_target="tpu_custom_call" | custom-call | tf_op jit(solution)/shard_map/pallas_call | solution.py:703
